TPU v7x, 32 devices: a whole 2x2x4 slice. The times are simulated.
32 devices in a mesh: seq: 8 (over z, x), rows: 4 (over y, core).
Axes of the slice: x: 2, y: 2, z: 4, core: 2. Of those that a mesh axis runs over, the one named last changes fastest.
Arguments:
- tokens: bfloat16 [4, 1024, 768], P('rows', 'seq'), may hold values from -6 to 6
- lengths: int32 [4, 8], P('rows'), may hold values from 1 to 968, as said below
- cotangent: bfloat16 [4, 1024, 768], P('rows', 'seq'), may hold values from -6 to 6
- w_query: bfloat16 [2, 768, 768], replicated, may hold values from -0.21875 to 0.21875
- b_query: bfloat16 [2, 768], replicated, may hold values from -3 to 3
- w_key: bfloat16 [2, 768, 768], replicated, may hold values from -0.21875 to 0.21875
- b_key: bfloat16 [2, 768], replicated, may hold values from -3 to 3
- w_value: bfloat16 [2, 768, 768], replicated, may hold values from -0.21875 to 0.21875
- b_value: bfloat16 [2, 768], replicated, may hold values from -0.059814453 to 0.059814453
- w_out: bfloat16 [2, 768, 768], replicated, may hold values from -1 to 1
- b_out: bfloat16 [2, 768], replicated, may hold values from -2 to 2
- norm1_gain: bfloat16 [2, 768], replicated, may hold values from 0.5 to 1.5
- norm1_bias: bfloat16 [2, 768], replicated, may hold values from -2 to 2
- w_inner: bfloat16 [2, 768, 3072], replicated, may hold values from -0.21875 to 0.21875
- b_inner: bfloat16 [2, 3072], replicated, may hold values from -3 to 3
- w_outer: bfloat16 [2, 3072, 768], replicated, may hold values from -0.109375 to 0.109375
- b_outer: bfloat16 [2, 768], replicated, may hold values from -2 to 2
- norm2_gain: bfloat16 [2, 768], replicated, may hold values from 0.5 to 1.5
- norm2_bias: bfloat16 [2, 768], replicated, may hold values from -2 to 2
Outputs:
- output: bfloat16 [4, 1024, 768], P('rows', 'seq')
- tokens_grad: bfloat16 [4, 1024, 768], P('rows', 'seq')
- w_query_grad: float32 [2, 768, 768], P(None, 'seq', 'rows')
- b_query_grad: float32 [2, 768], P(None, 'seq')
- w_key_grad: float32 [2, 768, 768], P(None, 'seq', 'rows')
- b_key_grad: float32 [2, 768], P(None, 'seq')
- w_value_grad: float32 [2, 768, 768], P(None, 'seq', 'rows')
- b_value_grad: float32 [2, 768], P(None, 'seq')
- w_out_grad: float32 [2, 768, 768], P(None, 'seq', 'rows')
- b_out_grad: float32 [2, 768], P(None, 'seq')
- norm1_gain_grad: float32 [2, 768], P(None, 'seq')
- norm1_bias_grad: float32 [2, 768], P(None, 'seq')
- w_inner_grad: float32 [2, 768, 3072], P(None, 'seq', 'rows')
- b_inner_grad: float32 [2, 3072], P(None, 'seq')
- w_outer_grad: float32 [2, 3072, 768], P(None, 'seq', 'rows')
- b_outer_grad: float32 [2, 768], P(None, 'seq')
- norm2_gain_grad: float32 [2, 768], P(None, 'seq')
- norm2_bias_grad: float32 [2, 768], P(None, 'seq')
Inputs may be any that keep to these rules, and one draw needn't show every extreme that they name: In every row the 8 lengths are positive and add up to 1024; one document of each row, never the first or the last, has exactly the largest length, and some document has length 1.
All inputs are finite; a program needn't handle non-finite values.
Results may differ from a plain program's by a relative error of at most 0.035.
Values may be sent and summed in bfloat16 or wider, within the bound.
No kernel may reach another device: no remote copies, remote signals or barrier semaphores. Data moves between devices by JAX's collectives and lax.ppermute only.
A program may use at most 448 MiB of HBM per device.

v0:
```python
import jax
import jax.numpy as jnp
from jax import lax
from jax.sharding import PartitionSpec as P

D = 768
HEADS = 12
HEAD_DIM = 64
LAYERS = 2


NEG_FILL = -1e30
NORM_EPS = 1e-12


def for_sending(array):

    def short(part):
        return part.astype(jnp.bfloat16) if part.dtype == jnp.float32 else part

    return jax.tree.map(short, array)


def doc_layout(lengths_row, index):
    ends = jnp.cumsum(lengths_row, dtype=jnp.int32)
    passed = (index[:, None] >= ends[None, :]).astype(jnp.int32)
    segment = jnp.sum(passed, axis=1, dtype=jnp.int32)
    begin = jnp.sum(passed * lengths_row[None, :], axis=1, dtype=jnp.int32)
    return (segment, (index - begin).astype(jnp.int32))


def segments_of(lengths_row, start, rows):
    return doc_layout(lengths_row, start + jnp.arange(rows, dtype=jnp.int32))[0]


def rotary_tables(position):
    pairs = jnp.arange(HEAD_DIM // 2, dtype=jnp.int32).astype(jnp.float32)
    inverse = jnp.power(jnp.float32(10000.0), -2.0 * pairs / HEAD_DIM)
    angle = position.astype(jnp.float32)[:, None] * inverse[None, :]
    cosine = jnp.tile(jnp.repeat(jnp.cos(angle), 2, axis=1), (1, HEADS))
    sine = jnp.tile(jnp.repeat(jnp.sin(angle), 2, axis=1), (1, HEADS))
    return (cosine, sine)


def rotate_pairs(values):
    shaped = values.reshape(values.shape[:-1] + (values.shape[-1] // 2, 2))
    return jnp.stack([-shaped[..., 1], shaped[..., 0]], axis=-1).reshape(values.shape)


def apply_rotary(values, cosine, sine):
    return values * cosine + rotate_pairs(values) * sine


def undo_rotary(grads, cosine, sine):
    return grads * cosine - rotate_pairs(grads * sine)


def norm_forward(values, gain, bias):
    centered = values - jnp.mean(values, axis=-1, keepdims=True)
    rstd = lax.rsqrt(jnp.mean(centered * centered, axis=-1, keepdims=True) + NORM_EPS)
    normed = centered * rstd
    return (normed * gain.astype(jnp.float32) + bias.astype(jnp.float32), normed, rstd)


def norm_backward(grad, normed, rstd, gain):
    scaled = grad * gain.astype(jnp.float32)
    centered = scaled - jnp.mean(scaled, axis=-1, keepdims=True)
    values_grad = rstd * (centered - normed * jnp.mean(scaled * normed, axis=-1, keepdims=True))
    return (values_grad, jnp.sum(grad * normed, axis=0), jnp.sum(grad, axis=0))


def project(inputs_b, weight, bias):
    return jnp.dot(inputs_b, weight, preferred_element_type=jnp.float32) + bias.astype(jnp.float32)


def back_project(grad_b, weight):
    return lax.dot_general(
        grad_b, weight, (((1,), (1,)), ((), ())), preferred_element_type=jnp.float32
    )


def weight_grad(left_b, right_b):
    return jnp.einsum("ti,tj->ij", left_b, right_b, preferred_element_type=jnp.float32)


def head_split(values):
    return values.reshape(values.shape[0], HEADS, HEAD_DIM)


def masked_scores(left_b, right_b, left_segment, right_segment):
    scores = jnp.einsum(
        "qhd,khd->hqk", head_split(left_b), head_split(right_b), preferred_element_type=jnp.float32
    ) * HEAD_DIM ** (-0.5)
    same = (left_segment[:, None] == right_segment[None, :])[None]
    return jnp.where(same, scores, NEG_FILL)


def layer_forward(current, weights, lengths_row, own_segment, cosine, sine):
    (
        w_query,
        b_query,
        w_key,
        b_key,
        w_value,
        b_value,
        w_out,
        b_out,
        gain_one,
        bias_one,
        w_inner,
        b_inner,
        w_outer,
        b_outer,
        gain_two,
        bias_two,
    ) = weights
    count = current.shape[0]
    inputs_b = current.astype(jnp.bfloat16)
    query_b = apply_rotary(project(inputs_b, w_query, b_query), cosine, sine).astype(jnp.bfloat16)
    key_b = apply_rotary(project(inputs_b, w_key, b_key), cosine, sine).astype(jnp.bfloat16)
    value_b = project(inputs_b, w_value, b_value).astype(jnp.bfloat16)
    start_values = jnp.zeros((count, HEADS, HEAD_DIM), jnp.float32)
    kept = {}
    piece = jax.tree.map(lambda a: lax.all_gather(a, "seq", axis=0, tiled=True), key_b)
    top = jnp.full((HEADS, count), NEG_FILL, jnp.float32)
    total = jnp.zeros((HEADS, count), jnp.float32)
    scores = masked_scores(
        query_b, piece, own_segment, segments_of(lengths_row, jnp.int32(0), piece.shape[0])
    )
    fresh = jnp.maximum(top, jnp.max(scores, axis=2))
    total = total * jnp.exp(top - fresh) + jnp.sum(jnp.exp(scores - fresh[:, :, None]), axis=2)
    top, total = (fresh, total)
    log_total = top + jnp.log(total)
    keys_piece = lax.all_gather(key_b, "seq", axis=0, tiled=True)
    values_piece = lax.all_gather(value_b, "seq", axis=0, tiled=True)
    scores = masked_scores(
        query_b,
        keys_piece,
        own_segment,
        segments_of(lengths_row, jnp.int32(0), keys_piece.shape[0]),
    )
    prob = jnp.exp(scores - log_total[:, :, None]).astype(jnp.bfloat16)
    attn = start_values + jnp.einsum(
        "hqk,khd->qhd", prob, head_split(values_piece), preferred_element_type=jnp.float32
    )
    attn = attn.reshape(count, D)
    attn_b = attn.astype(jnp.bfloat16)
    hidden, normed_one, rstd_one = norm_forward(
        current + project(attn_b, w_out, b_out), gain_one, bias_one
    )
    hidden_b = hidden.astype(jnp.bfloat16)
    inner = project(hidden_b, w_inner, b_inner)
    active_b = jax.nn.gelu(inner, approximate=False).astype(jnp.bfloat16)
    result, normed_two, rstd_two = norm_forward(
        hidden + project(active_b, w_outer, b_outer), gain_two, bias_two
    )
    kept.update(
        {
            "inputs": inputs_b,
            "query": query_b,
            "key": key_b,
            "value": value_b,
            "log_total": log_total,
            "attn": attn,
            "attn_b": attn_b,
            "normed_one": normed_one,
            "rstd_one": rstd_one,
            "hidden_b": hidden_b,
            "inner": inner,
            "active_b": active_b,
            "normed_two": normed_two,
            "rstd_two": rstd_two,
        }
    )
    return (result, kept)


def layer_backward(grad, kept, weights, lengths_row, own_segment, cosine, sine):
    (
        w_query,
        b_query,
        w_key,
        b_key,
        w_value,
        b_value,
        w_out,
        b_out,
        gain_one,
        bias_one,
        w_inner,
        b_inner,
        w_outer,
        b_outer,
        gain_two,
        bias_two,
    ) = weights
    count = grad.shape[0]
    scale = HEAD_DIM ** (-0.5)
    pre_two_grad, gain_two_grad, bias_two_grad = norm_backward(
        grad, kept["normed_two"], kept["rstd_two"], gain_two
    )
    outer_grad = pre_two_grad.astype(jnp.bfloat16)
    w_outer_grad = weight_grad(kept["active_b"], outer_grad)
    b_outer_grad = jnp.sum(outer_grad.astype(jnp.float32), axis=0)
    active_grad = back_project(outer_grad, w_outer)
    unused, gelu_back = jax.vjp(lambda inner: jax.nn.gelu(inner, approximate=False), kept["inner"])
    inner_grad = gelu_back(active_grad)[0].astype(jnp.bfloat16)
    w_inner_grad = weight_grad(kept["hidden_b"], inner_grad)
    b_inner_grad = jnp.sum(inner_grad.astype(jnp.float32), axis=0)
    hidden_grad = pre_two_grad + back_project(inner_grad, w_inner)
    pre_one_grad, gain_one_grad, bias_one_grad = norm_backward(
        hidden_grad, kept["normed_one"], kept["rstd_one"], gain_one
    )
    branch_grad = pre_one_grad.astype(jnp.bfloat16)
    w_out_grad = weight_grad(kept["attn_b"], branch_grad)
    b_out_grad = jnp.sum(branch_grad.astype(jnp.float32), axis=0)
    attn_grad = back_project(branch_grad, w_out).astype(jnp.bfloat16)
    delta = jnp.sum(head_split(attn_grad.astype(jnp.float32) * kept["attn"]), axis=2)
    log_total = kept["log_total"]
    grad_heads = head_split(attn_grad)
    start_query = jnp.zeros((count, HEADS, HEAD_DIM), jnp.float32)
    keys_piece = lax.all_gather(for_sending(kept["key"]), "seq", axis=0, tiled=True)
    values_piece = lax.all_gather(for_sending(kept["value"]), "seq", axis=0, tiled=True)
    scores = masked_scores(
        kept["query"],
        keys_piece,
        own_segment,
        segments_of(lengths_row, jnp.int32(0), keys_piece.shape[0]),
    )
    prob = jnp.exp(scores - log_total[:, :, None])
    prob_grad = jnp.einsum(
        "qhd,khd->hqk", grad_heads, head_split(values_piece), preferred_element_type=jnp.float32
    )
    score_grad = (prob * (prob_grad - delta.T[:, :, None]) * scale).astype(jnp.bfloat16)
    query_acc = start_query + jnp.einsum(
        "hqk,khd->qhd", score_grad, head_split(keys_piece), preferred_element_type=jnp.float32
    )
    query_in = undo_rotary(query_acc.reshape(count, D), cosine, sine).astype(jnp.bfloat16)
    whole_total, whole_delta = (
        lax.all_gather(log_total.T, "seq", axis=0, tiled=True),
        lax.all_gather(delta, "seq", axis=0, tiled=True),
    )
    own_values = head_split(kept["value"])
    zeros_heads = jnp.zeros((count, HEADS, HEAD_DIM), jnp.float32)
    start = jnp.int32(0)
    key_acc = zeros_heads
    value_acc = zeros_heads
    query_piece = lax.all_gather(for_sending(kept["query"]), "seq", axis=0, tiled=True)
    grad_piece = lax.all_gather(attn_grad, "seq", axis=0, tiled=True)
    rows = query_piece.shape[0]
    total_piece = lax.dynamic_slice_in_dim(whole_total, start, rows, 0)
    delta_piece = lax.dynamic_slice_in_dim(whole_delta, start, rows, 0)
    scores = masked_scores(
        query_piece, kept["key"], segments_of(lengths_row, start, rows), own_segment
    )
    prob = jnp.exp(scores - total_piece.T[:, :, None])
    piece_heads = head_split(grad_piece)
    prob_grad = jnp.einsum(
        "qhd,khd->hqk", piece_heads, own_values, preferred_element_type=jnp.float32
    )
    score_grad = (prob * (prob_grad - delta_piece.T[:, :, None]) * scale).astype(jnp.bfloat16)
    key_acc = key_acc + jnp.einsum(
        "hqk,qhd->khd", score_grad, head_split(query_piece), preferred_element_type=jnp.float32
    )
    value_acc = value_acc + jnp.einsum(
        "hqk,qhd->khd", prob.astype(jnp.bfloat16), piece_heads, preferred_element_type=jnp.float32
    )
    key_acc, value_acc = (key_acc, value_acc)
    key_in = undo_rotary(key_acc.reshape(count, D), cosine, sine).astype(jnp.bfloat16)
    value_in = value_acc.reshape(count, D).astype(jnp.bfloat16)
    inputs_b = kept["inputs"]
    input_grad = (
        pre_one_grad
        + back_project(query_in, w_query)
        + back_project(key_in, w_key)
        + back_project(value_in, w_value)
    )
    grads = (
        weight_grad(inputs_b, query_in),
        jnp.sum(query_in.astype(jnp.float32), axis=0),
        weight_grad(inputs_b, key_in),
        jnp.sum(key_in.astype(jnp.float32), axis=0),
        weight_grad(inputs_b, value_in),
        jnp.sum(value_in.astype(jnp.float32), axis=0),
        w_out_grad,
        b_out_grad,
        gain_one_grad,
        bias_one_grad,
        w_inner_grad,
        b_inner_grad,
        w_outer_grad,
        b_outer_grad,
        gain_two_grad,
        bias_two_grad,
    )
    return (input_grad, grads)


def regroup(mats, vecs):
    return (
        mats[0],
        vecs[0],
        mats[1],
        vecs[1],
        mats[2],
        vecs[2],
        mats[3],
        vecs[3],
        vecs[4],
        vecs[5],
        mats[4],
        vecs[6],
        mats[5],
        vecs[7],
        vecs[8],
        vecs[9],
    )


def reduce_stacked(grads):
    shares = lax.psum_scatter(grads, "seq", scatter_dimension=1, tiled=True)
    mats = (
        lax.psum_scatter(
            shares[0].astype(jnp.bfloat16), "rows", scatter_dimension=2, tiled=True
        ).astype(jnp.float32),
        lax.psum_scatter(
            shares[2].astype(jnp.bfloat16), "rows", scatter_dimension=2, tiled=True
        ).astype(jnp.float32),
        lax.psum_scatter(
            shares[4].astype(jnp.bfloat16), "rows", scatter_dimension=2, tiled=True
        ).astype(jnp.float32),
        lax.psum_scatter(
            shares[6].astype(jnp.bfloat16), "rows", scatter_dimension=2, tiled=True
        ).astype(jnp.float32),
        lax.psum_scatter(
            shares[10].astype(jnp.bfloat16), "rows", scatter_dimension=2, tiled=True
        ).astype(jnp.float32),
        lax.psum_scatter(
            shares[12].astype(jnp.bfloat16), "rows", scatter_dimension=2, tiled=True
        ).astype(jnp.float32),
    )
    vecs = lax.psum(
        (
            shares[1],
            shares[3],
            shares[5],
            shares[7],
            shares[8],
            shares[9],
            shares[11],
            shares[13],
            shares[14],
            shares[15],
        ),
        "rows",
    )
    return regroup(mats, vecs)


def body(
    tokens,
    lengths,
    cotangent,
    w_query,
    b_query,
    w_key,
    b_key,
    w_value,
    b_value,
    w_out,
    b_out,
    norm1_gain,
    norm1_bias,
    w_inner,
    b_inner,
    w_outer,
    b_outer,
    norm2_gain,
    norm2_bias,
):
    count = tokens.shape[1]
    lengths_row = lengths[0]
    own_index = lax.axis_index("seq") * count + jnp.arange(count, dtype=jnp.int32)
    own_segment, own_position = doc_layout(lengths_row, own_index)
    cosine, sine = rotary_tables(own_position)
    params = (
        w_query,
        b_query,
        w_key,
        b_key,
        w_value,
        b_value,
        w_out,
        b_out,
        norm1_gain,
        norm1_bias,
        w_inner,
        b_inner,
        w_outer,
        b_outer,
        norm2_gain,
        norm2_bias,
    )
    current = tokens[0].astype(jnp.float32)
    saved = []
    for layer in range(LAYERS):
        weights = tuple((param[layer] for param in params))
        current, kept = layer_forward(current, weights, lengths_row, own_segment, cosine, sine)
        saved.append(kept)
    grad = cotangent[0].astype(jnp.float32)
    by_layer = [None] * LAYERS
    for layer in range(LAYERS - 1, -1, -1):
        weights = tuple((param[layer] for param in params))
        grad, layer_grads = layer_backward(
            grad, saved[layer], weights, lengths_row, own_segment, cosine, sine
        )
        by_layer[layer] = layer_grads
    stacked = tuple(
        (
            jnp.stack([by_layer[layer][member] for layer in range(LAYERS)])
            for member in range(len(params))
        )
    )
    summed = reduce_stacked(stacked)
    return (current.astype(jnp.bfloat16)[None], grad.astype(jnp.bfloat16)[None]) + tuple(summed)


def solution(mesh):
    placed = (
        P("rows", "seq", None),
        P("rows", None),
        P("rows", "seq", None),
        P(),
        P(),
        P(),
        P(),
        P(),
        P(),
        P(),
        P(),
        P(),
        P(),
        P(),
        P(),
        P(),
        P(),
        P(),
        P(),
    )
    return jax.shard_map(
        body,
        mesh=mesh,
        in_specs=placed,
        out_specs=(
            P("rows", "seq", None),
            P("rows", "seq", None),
            P(None, "seq", "rows"),
            P(None, "seq"),
            P(None, "seq", "rows"),
            P(None, "seq"),
            P(None, "seq", "rows"),
            P(None, "seq"),
            P(None, "seq", "rows"),
            P(None, "seq"),
            P(None, "seq"),
            P(None, "seq"),
            P(None, "seq", "rows"),
            P(None, "seq"),
            P(None, "seq", "rows"),
            P(None, "seq"),
            P(None, "seq"),
            P(None, "seq"),
        ),
        check_vma=False,
    )
```

profile of v0, /device:TPU:0, one launch (start us, length us, event | category | flops | bytes accessed | tf_op | source)
XLA Modules:
  0.0 2318.1 jit_solution(14383364145779844649)
XLA Ops:
  26.8 40.4 %all-gather.11.cloned.1.call-done = bf16[1024,768]{1,0:T(8,128)(2,1)} async-done(((bf16[128,768]{1,0:T(8,128)(2,1)}), bf16[1024,768]{1,0:T(8,128)(2,1)}) %all-gather.11.cloned.1.call-update) | async-done | bytes 1572880 | tf_op jit(solution)/shard_map/all_gather | solution.py:134
  73.0 40.1 %all-gather.9.cloned.1.call-done = bf16[1024,768]{1,0:T(8,128)(2,1)} async-done(((bf16[128,768]{1,0:T(8,128)(2,1)}), bf16[1024,768]{1,0:T(8,128)(2,1)}) %all-gather.9.cloned.1.call-update) | async-done | bytes 1572880 | tf_op jit(solution)/shard_map/all_gather | solution.py:135
  155.7 40.1 %all-gather.15.cloned.1.call-done = bf16[1024,768]{1,0:T(8,128)(2,1)} async-done(((bf16[128,768]{1,0:T(8,128)(2,1)}), bf16[1024,768]{1,0:T(8,128)(2,1)}) %all-gather.15.cloned.1.call-update) | async-done | bytes 1572880 | tf_op jit(solution)/shard_map/all_gather | solution.py:134
  203.8 37.6 %all-gather.13.cloned.1.call-done = bf16[1024,768]{1,0:T(8,128)(2,1)} async-done(((bf16[128,768]{1,0:T(8,128)(2,1)}), bf16[1024,768]{1,0:T(8,128)(2,1)}) %all-gather.13.cloned.1.call-update) | async-done | bytes 1572880 | tf_op jit(solution)/shard_map/all_gather | solution.py:135
  294.9 32.2 %all_gather.49 = f32[1024,12]{0,1:T(8,128)} all-gather(f32[128,12]{0,1:T(8,128)} %reduce_sum.436), channel_id=1, replica_groups=mesh['seq'=8,'rows'=4] {'seq'}, dimensions={0}, use_global_device_ids=true | all-gather | bytes 55296 | tf_op jit(solution)/shard_map/all_gather | solution.py:241
  327.1 32.6 %all_gather.47 = f32[1024,12]{0,1:T(8,128)} all-gather(f32[128,12]{0,1:T(8,128)} %fusion.194), channel_id=1, replica_groups=mesh['seq'=8,'rows'=4] {'seq'}, dimensions={0}, use_global_device_ids=true | all-gather | bytes 55296 | tf_op jit(solution)/shard_map/all_gather | solution.py:240
  446.8 32.4 %all_gather.51 = f32[1024,12]{0,1:T(8,128)} all-gather(f32[128,12]{0,1:T(8,128)S(1)} %fusion.190), channel_id=1, replica_groups=mesh['seq'=8,'rows'=4] {'seq'}, dimensions={0}, use_global_device_ids=true | all-gather | bytes 55296 | tf_op jit(solution)/shard_map/all_gather | solution.py:240
  507.4 32.3 %all_gather.53 = f32[1024,12]{0,1:T(8,128)} all-gather(f32[128,12]{0,1:T(8,128)S(1)} %reduce_sum.442), channel_id=1, replica_groups=mesh['seq'=8,'rows'=4] {'seq'}, dimensions={0}, use_global_device_ids=true | all-gather | bytes 55296 | tf_op jit(solution)/shard_map/all_gather | solution.py:241
  607.7 665.7 %all-reduce.10 = (bf16[2,768,768]{2,0,1:T(2,128)(2,1)}, bf16[2,768,768]{2,0,1:T(2,128)(2,1)}, bf16[2,768,768]{2,0,1:T(2,128)(2,1)S(1)}) all-reduce(f32[2,768,768]{2,0,1:T(2,128)} %copy.248, f32[2,768,768]{2,0,1:T(2,128)} %copy.250, f32[2,768,768]{2,0,1:T(2,128)} %copy.252), channel_id=2, replica_groups=mesh['seq'=8,'rows'=4] {'seq'}, use_global_device_ids=true, to_apply=%region_26.27.clone | all-reduce | flops 3538944 | bytes 21233664
  1274.5 29.6 %copy.261 = bf16[2,96,768]{0,1,2:T(8,128)(2,1)} copy(bf16[2,96,768]{2,0,1:T(2,128)(2,1)S(1)} %dynamic-slice_convert_fusion.2) | data formatting | bytes 589824
  1334.6 29.6 %copy.265 = bf16[2,96,768]{0,1,2:T(8,128)(2,1)} copy(bf16[2,96,768]{2,0,1:T(2,128)(2,1)S(1)} %dynamic-slice_convert_fusion.1) | data formatting | bytes 589824
  1393.6 29.6 %copy.269 = bf16[2,96,768]{0,1,2:T(8,128)(2,1)} copy(bf16[2,96,768]{2,0,1:T(2,128)(2,1)S(1)} %dynamic-slice_convert_fusion) | data formatting | bytes 589824
  1460.1 45.8 %reduce-scatter.49.cloned.1.call-done = f32[2,96,3072]{2,1,0:T(8,128)} async-done(((f32[2,768,3072]{2,1,0:T(8,128)}), f32[2,96,3072]{2,1,0:T(8,128)}) %reduce-scatter.49.cloned.1.call-update) | async-done | bytes 2359312 | tf_op jit(solution)/shard_map/reduce_scatter | solution.py:321
  1510.1 59.4 %reduce-scatter.69.cloned.1.call-done = f32[96,2]{1,0:T(8,128)} async-done(((f32[768,2]{1,0:T(8,128)}), f32[96,2]{1,0:T(8,128)}) %reduce-scatter.69.cloned.1.call-update) | async-done | bytes 784
  1570.4 62.9 %reduce-scatter.71.cloned.1.call-done = f32[96,2]{1,0:T(8,128)} async-done(((f32[768,2]{1,0:T(8,128)}), f32[96,2]{1,0:T(8,128)}) %reduce-scatter.71.cloned.1.call-update) | async-done | bytes 784
  1634.2 62.7 %reduce-scatter.73.cloned.1.call-done = f32[96,2]{1,0:T(8,128)} async-done(((f32[768,2]{1,0:T(8,128)}), f32[96,2]{1,0:T(8,128)}) %reduce-scatter.73.cloned.1.call-update) | async-done | bytes 784
  1697.8 62.7 %reduce-scatter.77.cloned.1.call-done = f32[96,2]{1,0:T(8,128)} async-done(((f32[768,2]{1,0:T(8,128)}), f32[96,2]{1,0:T(8,128)}) %reduce-scatter.77.cloned.1.call-update) | async-done | bytes 784
  1761.9 62.2 %reduce-scatter.79.cloned.1.call-done = f32[96,2]{1,0:T(8,128)} async-done(((f32[768,2]{1,0:T(8,128)}), f32[96,2]{1,0:T(8,128)}) %reduce-scatter.79.cloned.1.call-update) | async-done | bytes 784
  1825.6 62.2 %reduce-scatter.81.cloned.1.call-done = f32[96,2]{1,0:T(8,128)} async-done(((f32[768,2]{1,0:T(8,128)}), f32[96,2]{1,0:T(8,128)}) %reduce-scatter.81.cloned.1.call-update) | async-done | bytes 784
  1889.2 65.7 %reduce-scatter.75.cloned.1.call-done = f32[384,2]{1,0:T(8,128)} async-done(((f32[3072,2]{1,0:T(8,128)}), f32[384,2]{1,0:T(8,128)}) %reduce-scatter.75.cloned.1.call-update) | async-done | bytes 3088
  1959.7 59.7 %reduce-scatter.57.cloned.1.call-done = f32[96,2]{1,0:T(8,128)} async-done(((f32[768,2]{1,0:T(8,128)}), f32[96,2]{1,0:T(8,128)}) %reduce-scatter.57.cloned.1.call-update) | async-done | bytes 784
  2020.3 63.1 %reduce-scatter.61.cloned.1.call-done = f32[96,2]{1,0:T(8,128)} async-done(((f32[768,2]{1,0:T(8,128)}), f32[96,2]{1,0:T(8,128)}) %reduce-scatter.61.cloned.1.call-update) | async-done | bytes 784
  2084.2 63.2 %reduce-scatter.65.cloned.1.call-done = f32[96,2]{1,0:T(8,128)} async-done(((f32[768,2]{1,0:T(8,128)}), f32[96,2]{1,0:T(8,128)}) %reduce-scatter.65.cloned.1.call-update) | async-done | bytes 784
  2242.7 37.9 %all-reduce.9.cloned.1.call-done = bf16[2,384,768]{1,0,2:T(2,128)(2,1)} async-done(((bf16[2,384,768]{1,0,2:T(2,128)(2,1)}), bf16[2,384,768]{1,0,2:T(2,128)(2,1)}) %all-reduce.9.cloned.1.call-update) | async-done | bytes 1179664
  (641 shorter events, 550.0 us)
Async XLA Ops:
  23.2 172.6 %all-gather.15.cloned.1.call-start = ((), (), s32[]{:S(2)}) async-start(), calls=%async_computation.21 | async-start | bytes 1769472 | tf_op jit(solution)/shard_map/all_gather | solution.py:134
  155.1 212.3 %all-gather.17.cloned.1.call-start = ((), (), s32[]{:S(2)}) async-start(), calls=%async_computation.22 | async-start | bytes 1769472 | tf_op jit(solution)/shard_map/all_gather | solution.py:248
  155.7 219.5 %all-gather.19.cloned.1.call-start = ((), (), s32[]{:S(2)}) async-start(), calls=%async_computation.23 | async-start | bytes 1769472 | tf_op jit(solution)/shard_map/all_gather | solution.py:249
  280.5 164.5 %all-gather.21.cloned.1.call-start = ((), (), s32[]{:S(2)}) async-start(), calls=%async_computation.24 | async-start | bytes 1769472 | tf_op jit(solution)/shard_map/all_gather | solution.py:248
  281.3 258.7 %all-gather.23.cloned.1.call-start = ((), (), s32[]{:S(2)}) async-start(), calls=%async_computation.25 | async-start | bytes 1769472 | tf_op jit(solution)/shard_map/all_gather | solution.py:249
  414.6 1037.9 %reduce-scatter.47.cloned.1.call-start = ((), (), s32[]{:S(2)}) async-start(), calls=%async_computation.26 | async-start | bytes 5308416 | tf_op jit(solution)/shard_map/reduce_scatter | solution.py:321
  419.2 1035.9 %reduce-scatter.53.cloned.1.call-start = ((), (), s32[]{:S(2)}) async-start(), calls=%async_computation.29 | async-start | bytes 21233664 | tf_op jit(solution)/shard_map/reduce_scatter | solution.py:321
  430.0 1075.9 %reduce-scatter.49.cloned.1.call-start = ((), (), s32[]{:S(2)}) async-start(), calls=%async_computation.27 | async-start | bytes 21233664 | tf_op jit(solution)/shard_map/reduce_scatter | solution.py:321
  441.2 1128.3 %reduce-scatter.69.cloned.1.call-start = ((), (), s32[]{:S(2)}) async-start(), calls=%async_computation.37 | async-start | bytes 442368
  499.4 1133.9 %reduce-scatter.71.cloned.1.call-start = ((), (), s32[]{:S(2)}) async-start(), calls=%async_computation.38 | async-start | bytes 442368
  501.1 1195.8 %reduce-scatter.73.cloned.1.call-start = ((), (), s32[]{:S(2)}) async-start(), calls=%async_computation.39 | async-start | bytes 442368
  502.2 1258.3 %reduce-scatter.77.cloned.1.call-start = ((), (), s32[]{:S(2)}) async-start(), calls=%async_computation.41 | async-start | bytes 442368
  503.3 1320.8 %reduce-scatter.79.cloned.1.call-start = ((), (), s32[]{:S(2)}) async-start(), calls=%async_computation.42 | async-start | bytes 442368
  504.4 1383.3 %reduce-scatter.81.cloned.1.call-start = ((), (), s32[]{:S(2)}) async-start(), calls=%async_computation.43 | async-start | bytes 442368
  507.3 1447.5 %reduce-scatter.75.cloned.1.call-start = ((), (), s32[]{:S(2)}) async-start(), calls=%async_computation.40 | async-start | bytes 1769472
  539.7 1479.7 %reduce-scatter.57.cloned.1.call-start = ((), (), s32[]{:S(2)}) async-start(), calls=%async_computation.31 | async-start | bytes 442368
  580.8 1502.6 %reduce-scatter.61.cloned.1.call-start = ((), (), s32[]{:S(2)}) async-start(), calls=%async_computation.33 | async-start | bytes 442368
  581.9 1565.5 %reduce-scatter.65.cloned.1.call-start = ((), (), s32[]{:S(2)}) async-start(), calls=%async_computation.35 | async-start | bytes 442368
  607.6 1562.9 %reduce-scatter.55.cloned.1.call-start = ((), (), s32[]{:S(2)}) async-start(), calls=%async_computation.30 | async-start | bytes 491520
  1333.3 860.7 %reduce-scatter.59.cloned.1.call-start = ((), (), s32[]{:S(2)}) async-start(), calls=%async_computation.32 | async-start | bytes 491520
  1393.4 824.1 %reduce-scatter.63.cloned.1.call-start = ((), (), s32[]{:S(2)}) async-start(), calls=%async_computation.34 | async-start | bytes 491520
  1452.4 788.5 %reduce-scatter.67.cloned.1.call-start = ((), (), s32[]{:S(2)}) async-start(), calls=%async_computation.36 | async-start | bytes 491520
  1455.0 825.6 %all-reduce.9.cloned.1.call-start = ((), (), s32[]{:S(2)}) async-start(), calls=%async_computation.44 | async-start | bytes 2359296
  1459.8 849.3 %reduce-scatter.51.cloned.1.call-start = ((), (), s32[]{:S(2)}) async-start(), calls=%async_computation.28 | async-start | bytes 1474560 | tf_op jit(solution)/shard_map/reduce_scatter | solution.py:335
  (164 other events, 3038.9 us)
Sparse Core Ops, SparseCore 0:
  20.4 46.8 all-gather.10
  70.0 42.9 all-gather.8
  152.8 42.9 all-gather.14
  198.4 42.9 all-gather.12
  243.5 42.9 all-gather.16
  288.5 43.2 all-gather.18
  334.0 43.1 all-gather.20
  414.7 43.7 all-gather.22
  462.1 94.5 reduce-scatter.46
  560.4 588.2 reduce-scatter.52
  1152.6 353.2 reduce-scatter.48
  1509.0 60.5 reduce-scatter.68
  1572.8 60.4 reduce-scatter.70
  1636.4 60.4 reduce-scatter.72
  1700.0 60.4 reduce-scatter.76
  1763.6 60.4 reduce-scatter.78
  1827.2 60.4 reduce-scatter.80
  1891.0 63.8 reduce-scatter.74
  1959.1 60.3 reduce-scatter.56
  2022.9 60.4 reduce-scatter.60
  2087.0 60.4 reduce-scatter.64
  2196.5 20.8 reduce-scatter.62
  2243.3 37.2 all-reduce.8
  2283.2 25.8 reduce-scatter.50
  (3 shorter events, 61.3 us)
where the time goes:
time: 2330 us; the launch traced here: 2320 us
  waiting for transfers between devices  922 us (40%)
  blocking collectives  806 us (35%)
  local copies, waits for them, and re-layouts  343 us (15%)
  matrix products  147 us (6%)
  other arithmetic  79.8 us (3%)
    unnamed x42, waiting for transfers between devices  691 us
    unnamed x1, blocking collectives  666 us
    unnamed x364, local copies, waits for them, and re-layouts  264 us
    all_gather x2, waiting for transfers between devices, layer_forward(): keys_piece = lax.all_gather(key_b, 'seq', axis=0, tiled=True)  80.5 us
    all_gather x2, waiting for transfers between devices, layer_forward(): values_piece = lax.all_gather(value_b, 'seq', axis=0, tiled=True)  77.7 us
    all_gather x2, blocking collectives, layer_backward(): lax.all_gather(log_total.T, 'seq', axis=0, tiled=True)  64.9 us
    all_gather x2, blocking collectives, layer_backward(): lax.all_gather(delta, 'seq', axis=0, tiled=True)  64.5 us
  transfers between devices with their start and end apart: 27, of which 21 were waited for; matrix products, arithmetic and copies ran while one was open for 22% of the time, Pallas kernels for 0%

commit v1 on v0

v1 whole, which is shorter than its diff:
```python
import functools

import jax
import jax.numpy as jnp
from jax import lax
from jax.experimental import pallas as pl
from jax.experimental.pallas import tpu as pltpu
from jax.sharding import PartitionSpec as P

D = 768
HEADS = 12
HEAD_DIM = 64
FF = 3072
LAYERS = 2
LANES = 128
PAIRS = D // LANES
CHUNK = D // 4
NEG_FILL = -1e30
NORM_EPS = 1e-12
SCALE = HEAD_DIM**-0.5
BF = jnp.bfloat16
F32 = jnp.float32
BOTH = ("seq", "rows")
MIB = 1 << 20

BQ, BK, BV, BO, G1, C1, BU, G2, C2 = range(9)
LSE_HI, LSE_LO, DELTA_HI, DELTA_LO = 0, 16, 32, 48


def dot(a, b):
    return jnp.dot(a, b, preferred_element_type=F32)


def dot_nt(a, b):
    return lax.dot_general(a, b, (((1,), (1,)), ((), ())), preferred_element_type=F32)


def call(kernel, name, grid, in_specs, out_specs, out_shape, args, flops, scratch=(), scalars=(), vmem=40):
    size = sum(a.size * a.dtype.itemsize for a in args) + sum(
        s.size * s.dtype.itemsize for s in jax.tree.leaves(out_shape)
    )
    return pl.pallas_call(
        kernel,
        name=name,
        grid_spec=pltpu.PrefetchScalarGridSpec(
            num_scalar_prefetch=len(scalars),
            grid=grid,
            in_specs=in_specs,
            out_specs=out_specs,
            scratch_shapes=list(scratch),
        ),
        out_shape=out_shape,
        compiler_params=pltpu.CompilerParams(
            dimension_semantics=("arbitrary",) * len(grid), vmem_limit_bytes=vmem * MIB
        ),
        cost_estimate=pl.CostEstimate(flops=int(flops), bytes_accessed=int(size), transcendentals=0),
    )(*scalars, *args)


def whole(array):
    return pl.BlockSpec(array.shape, lambda *_: (0,) * array.ndim)


def layer_block(array, layer):
    return pl.BlockSpec((None,) + array.shape[1:], lambda *_: (layer,) + (0,) * (array.ndim - 1))


def sds(shape, dtype):
    return jax.ShapeDtypeStruct(shape, dtype)


def lane_is_even(shape):
    return lax.broadcasted_iota(jnp.int32, shape, 1) % 2 == 0


def swap_pairs(v):
    return jnp.where(lane_is_even(v.shape), pltpu.roll(v, LANES - 1, 1), pltpu.roll(v, 1, 1))


def lanes(j):
    return slice(j * LANES, (j + 1) * LANES)


def qkv_kernel(x_ref, wq_ref, wk_ref, wv_ref, vec_ref, cos_ref, sin_ref, q_ref, k_ref, v_ref):
    x, cos, sin = x_ref[...], cos_ref[...], sin_ref[...]
    for w_ref, row, o_ref in ((wq_ref, BQ, q_ref), (wk_ref, BK, k_ref)):
        y = dot(x, w_ref[...]) + vec_ref[row : row + 1, :]
        for j in range(PAIRS):
            t = y[:, lanes(j)]
            o_ref[:, lanes(j)] = (t * cos + swap_pairs(t) * sin).astype(BF)
    v_ref[...] = (dot(x, wv_ref[...]) + vec_ref[BV : BV + 1, :]).astype(BF)


def project(rows, layer, wq, wk, wv, vec, cos, sin):
    total = rows.shape[0]
    block = min(256, total)
    tok = lambda w: pl.BlockSpec((block, w), lambda i: (i, 0))
    return call(
        qkv_kernel, "qkv", (total // block,),
        [tok(D)] + [layer_block(w, layer) for w in (wq, wk, wv, vec)] + [tok(LANES), tok(LANES)],
        [tok(D)] * 3, [sds((total, D), BF)] * 3,
        (rows, wq, wk, wv, vec, cos, sin), 6 * total * D * D,
    )


def over_chunks(total, body, carry):
    size = min(total, 1024)
    if size == total:
        return body(slice(None), carry)
    return lax.fori_loop(
        0, total // size, lambda i, c: body(pl.ds(pl.multiple_of(i * size, size), size), c), carry
    )


def two_heads(v):
    low = lax.broadcasted_iota(jnp.int32, v.shape, 1) < HEAD_DIM
    zero = jnp.zeros_like(v)
    return jnp.concatenate([jnp.where(low, v, zero), jnp.where(low, zero, v)], axis=0)


def join_heads(v):
    n = v.shape[0] // 2
    low = lax.broadcasted_iota(jnp.int32, (n, LANES), 1) < HEAD_DIM
    return jnp.where(low, v[:n], v[n:])


def attend_kernel(q_ref, k_ref, v_ref, own_ref, all_ref, attn_ref, lse_ref):
    pair = pl.program_id(0)
    n, total = q_ref.shape[0], k_ref.shape[0]
    q = two_heads(q_ref[...] * jnp.asarray(SCALE, BF))
    own = own_ref[...]

    def body(at, carry):
        top, tot, acc = carry
        same = own == all_ref[:, at]
        s = jnp.where(jnp.concatenate([same, same], axis=0), dot_nt(q, k_ref[at, :]), NEG_FILL)
        fresh = jnp.maximum(top, jnp.max(s, axis=1, keepdims=True))
        e = jnp.exp(s - fresh)
        keep = jnp.exp(top - fresh)
        tot = tot * keep + jnp.sum(e, axis=1, keepdims=True)
        acc = acc * keep + dot(e.astype(BF), v_ref[at, :])
        return fresh, tot, acc

    zero = jnp.zeros((2 * n, 1), F32)
    top, tot, acc = over_chunks(total, body, (zero + NEG_FILL, zero, jnp.zeros((2 * n, LANES), F32)))
    attn_ref[...] = join_heads(acc / tot)
    lse = top + jnp.log(tot)
    lane = lax.broadcasted_iota(jnp.int32, (n, LANES), 1)

    @pl.when(pair == 0)
    def _():
        lse_ref[...] = jnp.zeros_like(lse_ref)

    old = lse_ref[...]
    lse_ref[...] = jnp.where(lane == 2 * pair, lse[:n], jnp.where(lane == 2 * pair + 1, lse[n:], old))


def attend(q, k, v, own_seg, all_seg, n):
    total = k.shape[0]
    own = pl.BlockSpec((n, LANES), lambda p: (0, p))
    row = pl.BlockSpec((total, LANES), lambda p: (0, p))
    return call(
        attend_kernel, "attend", (PAIRS,),
        [own, row, row, whole(own_seg), whole(all_seg)],
        [own, pl.BlockSpec((n, LANES), lambda p: (0, 0))],
        [sds((n, D), F32), sds((n, LANES), F32)],
        (q, k, v, own_seg, all_seg), 4 * n * total * D * 2, vmem=56,
    )


def normalize(values):
    centered = values - jnp.mean(values, axis=-1, keepdims=True)
    rstd = lax.rsqrt(jnp.mean(centered * centered, axis=-1, keepdims=True) + NORM_EPS)
    return centered * rstd, rstd


FB = 768


def ffn_kernel(
    x_ref, attn_ref, wo_ref, wi_ref, bi_ref, wu_ref, vec_ref,
    out_ref, outb_ref, n1_ref, n2_ref, stat_ref, slope_ref, pack_ref,
    hid_ref, acc_ref,
):
    j = pl.program_id(0)
    lane = lax.broadcasted_iota(jnp.int32, stat_ref.shape, 1)

    @pl.when(j == 0)
    def _():
        attn_b = attn_ref[...].astype(BF)
        pack_ref[:, D : 2 * D] = attn_b
        branch = dot(attn_b, wo_ref[...]) + vec_ref[BO : BO + 1, :]
        n1, r1 = normalize(x_ref[...].astype(F32) + branch)
        hidden = n1 * vec_ref[G1 : G1 + 1, :] + vec_ref[C1 : C1 + 1, :]
        n1_ref[...] = n1
        stat_ref[...] = jnp.where(lane == 0, r1, 0.0)
        pack_ref[:, :D] = hidden.astype(BF)
        hid_ref[...] = hidden
        acc_ref[...] = jnp.zeros_like(acc_ref)

    inner = dot(pack_ref[:, :D], wi_ref[...]) + bi_ref[...]
    half = 0.5 + 0.5 * lax.erf(inner * (0.5**0.5))
    active = (inner * half).astype(BF)
    slope_ref[...] = half + inner * jnp.exp(-0.5 * inner * inner) * 0.3989422804014327
    pack_ref[:, pl.ds(pl.multiple_of(2 * D + j * FB, LANES), FB)] = active
    acc_ref[...] += dot(active, wu_ref[...])

    @pl.when(j == pl.num_programs(0) - 1)
    def _():
        n2, r2 = normalize(hid_ref[...] + acc_ref[...] + vec_ref[BU : BU + 1, :])
        out = n2 * vec_ref[G2 : G2 + 1, :] + vec_ref[C2 : C2 + 1, :]
        n2_ref[...] = n2
        stat_ref[...] = jnp.where(lane == 1, r2, stat_ref[...])
        out_ref[...] = out
        outb_ref[...] = out.astype(BF)


def feed_forward(x, attn, layer, wo, wi, bi, wu, vec):
    n = x.shape[0]
    fixed = lambda w: pl.BlockSpec((n, w), lambda j: (0, 0))
    return call(
        ffn_kernel, "ffn", (FF // FB,),
        [
            fixed(D), fixed(D), layer_block(wo, layer),
            pl.BlockSpec((None, D, FB), lambda j: (layer, 0, j)),
            pl.BlockSpec((None, 1, FB), lambda j: (layer, 0, j)),
            pl.BlockSpec((None, FB, D), lambda j: (layer, j, 0)),
            layer_block(vec, layer),
        ],
        [fixed(D)] * 4 + [fixed(LANES), pl.BlockSpec((n, FB), lambda j: (0, j)), fixed(2 * D + FF)],
        [sds((n, D), F32), sds((n, D), BF), sds((n, D), F32), sds((n, D), F32), sds((n, LANES), F32),
         sds((n, FF), F32), sds((n, 2 * D + FF), BF)],
        (x, attn, wo, wi, bi, wu, vec), 2 * n * (D * D + 2 * D * FF),
        scratch=[pltpu.VMEM((n, D), F32), pltpu.VMEM((n, D), F32)],
    )


def column_sum(v):
    return jnp.sum(v.astype(F32), axis=0, keepdims=True)


def norm_back(grad, normed, rstd, gain):
    scaled = grad * gain
    centered = scaled - jnp.mean(scaled, axis=-1, keepdims=True)
    return rstd * (centered - normed * jnp.mean(scaled * normed, axis=-1, keepdims=True))


def halves(v, c):
    part = [v[:, k * CHUNK : (k + 1) * CHUNK] for k in range(4)]
    even, odd = jnp.concatenate([part[0], part[2]], axis=1), jnp.concatenate([part[1], part[3]], axis=1)
    return jnp.where(c == 0, even, odd), jnp.where(c == 0, odd, even)


def hi_lo(v):
    hi = v.astype(BF)
    return hi, (v - hi.astype(F32)).astype(BF)


def ffn_back_kernel(
    place_ref, grad_ref, n1_ref, n2_ref, stat_ref, slope_ref, wu_ref, wi_ref, wo_ref, vec_ref, attn_ref, lse_ref,
    keep_ref, send_ref, keep_in_ref, send_in_ref, pre_ref, pack_ref, delta_ref, sums_ref, inner_sum_ref,
    two_ref, outer_ref, acc_ref,
):
    j = pl.program_id(0)
    c = place_ref[2]

    @pl.when(j == 0)
    def _():
        grad, n2 = grad_ref[...].astype(F32), n2_ref[...]
        sums_ref[0:1, :] = column_sum(grad * n2)
        sums_ref[1:2, :] = column_sum(grad)
        pre_two = norm_back(grad, n2, stat_ref[:, 1:2], vec_ref[G2 : G2 + 1, :])
        outer = pre_two.astype(BF)
        sums_ref[2:3, :] = column_sum(outer)
        two_ref[...] = pre_two
        outer_ref[...] = outer
        keep, send = halves(outer, c)
        keep_ref[:, : 2 * CHUNK] = keep
        send_ref[:, : 2 * CHUNK] = send
        acc_ref[...] = jnp.zeros_like(acc_ref)

    inner = (dot_nt(outer_ref[...], wu_ref[...]) * slope_ref[...]).astype(BF)
    inner_sum_ref[...] = column_sum(inner)

    @pl.when(j % 2 == c)
    def _():
        keep_in_ref[...] = inner

    @pl.when(j % 2 != c)
    def _():
        send_in_ref[...] = inner

    acc_ref[...] += dot_nt(inner, wi_ref[...])

    @pl.when(j == pl.num_programs(0) - 1)
    def _():
        grad, n1 = two_ref[...] + acc_ref[...], n1_ref[...]
        sums_ref[3:4, :] = column_sum(grad * n1)
        sums_ref[4:5, :] = column_sum(grad)
        pre_one = norm_back(grad, n1, stat_ref[:, 0:1], vec_ref[G1 : G1 + 1, :])
        pre_ref[...] = pre_one
        branch = pre_one.astype(BF)
        sums_ref[5:6, :] = column_sum(branch)
        sums_ref[6:8, :] = jnp.zeros((2, D), F32)
        keep, send = halves(branch, c)
        keep_ref[:, 2 * CHUNK :] = keep
        send_ref[:, 2 * CHUNK :] = send
        attn_grad = dot_nt(branch, wo_ref[...]).astype(BF)
        pack_ref[:, :D] = attn_grad
        feature = lax.broadcasted_iota(jnp.int32, (D, LANES), 0) // HEAD_DIM
        member = (feature == lax.broadcasted_iota(jnp.int32, (D, LANES), 1)).astype(BF)
        hi, lo = hi_lo(attn_grad.astype(F32) * attn_ref[...])
        delta = dot(hi, member) + dot(lo, member)
        delta_ref[...] = delta
        lse_hi, lse_lo = hi_lo(lse_ref[...])
        delta_hi, delta_lo = hi_lo(delta)
        extra = lse_hi.astype(F32)
        for v, at in ((lse_lo, LSE_LO), (delta_hi, DELTA_HI), (delta_lo, DELTA_LO)):
            extra = extra + pltpu.roll(v.astype(F32), at, 1)
        pack_ref[:, D:] = extra.astype(BF)


def feed_forward_back(spot, grad, kept, layer, wu, wi, wo, vec):
    n = grad.shape[0]
    assert FF // FB == 4
    fixed = lambda w: pl.BlockSpec((n, w), lambda j, s: (0, 0))
    args = (grad, kept["n1"], kept["n2"], kept["stat"], kept["slope"], wu, wi, wo, vec, kept["attn"], kept["lse"])
    return call(
        ffn_back_kernel, "ffn_back", (FF // FB,),
        [
            fixed(D), fixed(D), fixed(D), fixed(LANES),
            pl.BlockSpec((n, FB), lambda j, s: (0, j)),
            pl.BlockSpec((None, FB, D), lambda j, s: (layer, j, 0)),
            pl.BlockSpec((None, D, FB), lambda j, s: (layer, 0, j)),
            layer_block(wo, layer), layer_block(vec, layer), fixed(D), fixed(LANES),
        ],
        [
            fixed(4 * CHUNK), fixed(4 * CHUNK), pl.BlockSpec((n, FB), lambda j, s: (0, j // 2)), pl.BlockSpec((n, FB), lambda j, s: (0, j // 2)),
            fixed(D), fixed(D + LANES), fixed(LANES),
            pl.BlockSpec((8, D), lambda j, s: (0, 0)), pl.BlockSpec((1, FB), lambda j, s: (0, j)),
        ],
        [sds((n, 4 * CHUNK), BF)] * 2 + [sds((n, 2 * FB), BF)] * 2
        + [sds((n, D), F32), sds((n, D + LANES), BF), sds((n, LANES), F32), sds((8, D), F32), sds((1, FF), F32)],
        args, 2 * n * (D * D + 2 * D * FF),
        scratch=[pltpu.VMEM((n, D), F32), pltpu.VMEM((n, D), BF), pltpu.VMEM((n, D), F32)],
        scalars=(spot,),
    )


def unrotate(v, cos, sin):
    t = v * sin
    return v * cos + swap_pairs(t)


def lane_of(v, lane):
    at = lax.broadcasted_iota(jnp.int32, v.shape, 1)
    return jnp.sum(jnp.where(at == lane, v, 0.0), axis=1, keepdims=True)


def query_back_kernel(
    place_ref, q_ref, k_ref, v_ref, g_ref, lse_ref, delta_ref, own_ref, all_ref, cos_ref, sin_ref,
    dq_ref, keep_ref, send_ref, sum_ref,
    full_ref,
):
    pair = pl.program_id(0)
    n, total = q_ref.shape[0], k_ref.shape[0]
    q = two_heads(q_ref[...] * jnp.asarray(SCALE, BF))
    g = two_heads(g_ref[...])
    own = own_ref[...]
    lse = jnp.concatenate([lane_of(lse_ref[...], 2 * pair), lane_of(lse_ref[...], 2 * pair + 1)], axis=0)
    delta = jnp.concatenate([lane_of(delta_ref[...], 2 * pair), lane_of(delta_ref[...], 2 * pair + 1)], axis=0)

    def body(at, acc):
        same = own == all_ref[:, at]
        k = k_ref[at, :]
        s = jnp.where(jnp.concatenate([same, same], axis=0), dot_nt(q, k) - lse, NEG_FILL)
        ds = (jnp.exp(s) * (dot_nt(g, v_ref[at, :]) - delta)).astype(BF)
        return acc + dot(ds, k)

    acc = join_heads(over_chunks(total, body, jnp.zeros((2 * n, LANES), F32))) * SCALE
    dq = unrotate(acc, cos_ref[...], sin_ref[...]).astype(BF)
    dq_ref[...] = dq
    sum_ref[...] = column_sum(dq)
    full_ref[:, pl.ds(pl.multiple_of(pair * LANES, LANES), LANES)] = dq

    @pl.when(pair == pl.num_programs(0) - 1)
    def _():
        keep_ref[...], send_ref[...] = halves(full_ref[...], place_ref[2])


def query_back(spot, q, k, v, pack, lse, delta, own_seg, all_seg, cos, sin):
    n, total = pack.shape[0], k.shape[0]
    own = pl.BlockSpec((n, LANES), lambda p, s: (0, p))
    row = pl.BlockSpec((total, LANES), lambda p, s: (0, p))
    fixed = lambda w: pl.BlockSpec((n, w), lambda p, s: (0, 0))
    return call(
        query_back_kernel, "query_back", (PAIRS,),
        [own, row, row, own, fixed(LANES), fixed(LANES), whole(own_seg), whole(all_seg), fixed(LANES), fixed(LANES)],
        [own, fixed(2 * CHUNK), fixed(2 * CHUNK), pl.BlockSpec((1, LANES), lambda p, s: (0, p))],
        [sds((n, D), BF), sds((n, 2 * CHUNK), BF), sds((n, 2 * CHUNK), BF), sds((1, D), F32)],
        (q, k, v, pack, lse, delta, own_seg, all_seg, cos, sin), 6 * n * total * D * 2,
        scratch=[pltpu.VMEM((n, D), BF)], scalars=(spot,), vmem=56,
    )


def key_back_kernel(
    place_ref, k_ref, v_ref, q_ref, g_ref, extra_ref, own_ref, all_ref, cos_ref, sin_ref,
    dk_ref, dv_ref, keep_ref, send_ref, dk_sum_ref, dv_sum_ref,
    rows_ref, full_k_ref, full_v_ref,
):
    pair = pl.program_id(0)
    n, total = k_ref.shape[0], q_ref.shape[0]

    @pl.when(pair == 0)
    def _():
        row = lax.broadcasted_iota(jnp.int32, (32, LANES), 0)
        lane = lax.broadcasted_iota(jnp.int32, (32, LANES), 1)
        first = jnp.where(row < 16, LSE_HI, DELTA_HI - 16) + row
        pick = ((lane == first) | (lane == first + 16)).astype(BF)

        def fill(at, carry):
            rows_ref[:, at] = dot_nt(pick, extra_ref[at, :])
            return carry

        over_chunks(total, fill, 0)

    k = two_heads(k_ref[...] * jnp.asarray(SCALE, BF))
    v = two_heads(v_ref[...])
    own = own_ref[...]

    def body(at, carry):
        dk, dv = carry
        same = own == all_ref[:, at]
        q, g = q_ref[at, :], g_ref[at, :]
        s, dp = dot_nt(k, q), dot_nt(v, g)
        probs, ds = [], []
        for h in range(2):
            part = slice(h * n, (h + 1) * n)
            lse = rows_ref[pl.ds(2 * pair + h, 1), at]
            delta = rows_ref[pl.ds(16 + 2 * pair + h, 1), at]
            p = jnp.exp(jnp.where(same, s[part] - lse, NEG_FILL))
            probs.append(p.astype(BF))
            ds.append((p * (dp[part] - delta)).astype(BF))
        dk = dk + dot(jnp.concatenate(ds, axis=0), q)
        dv = dv + dot(jnp.concatenate(probs, axis=0), g)
        return dk, dv

    zero = jnp.zeros((2 * n, LANES), F32)
    dk, dv = over_chunks(total, body, (zero, zero))
    dk = unrotate(join_heads(dk) * SCALE, cos_ref[...], sin_ref[...]).astype(BF)
    dv = join_heads(dv).astype(BF)
    dk_ref[...] = dk
    dv_ref[...] = dv
    dk_sum_ref[...] = column_sum(dk)
    dv_sum_ref[...] = column_sum(dv)
    at = pl.ds(pl.multiple_of(pair * LANES, LANES), LANES)
    full_k_ref[:, at] = dk
    full_v_ref[:, at] = dv

    @pl.when(pair == pl.num_programs(0) - 1)
    def _():
        c = place_ref[2]
        k_keep, k_send = halves(full_k_ref[...], c)
        v_keep, v_send = halves(full_v_ref[...], c)
        for o_ref, kk, vv in ((keep_ref, k_keep, v_keep), (send_ref, k_send, v_send)):
            parts = [u[:, y * CHUNK : (y + 1) * CHUNK] for y in range(2) for u in (kk, vv)]
            o_ref[...] = jnp.concatenate(parts, axis=1)


def key_back(spot, k, v, q, pack_all, own_seg, all_seg, cos, sin, n):
    total = q.shape[0]
    own = pl.BlockSpec((n, LANES), lambda p, s: (0, p))
    row = pl.BlockSpec((total, LANES), lambda p, s: (0, p))
    fixed = lambda w: pl.BlockSpec((n, w), lambda p, s: (0, 0))
    one = pl.BlockSpec((1, LANES), lambda p, s: (0, p))
    return call(
        key_back_kernel, "key_back", (PAIRS,),
        [own, own, row, row, pl.BlockSpec((total, LANES), lambda p, s: (0, PAIRS)),
         whole(own_seg), whole(all_seg), fixed(LANES), fixed(LANES)],
        [own, own, fixed(4 * CHUNK), fixed(4 * CHUNK), one, one],
        [sds((n, D), BF), sds((n, D), BF), sds((n, 4 * CHUNK), BF), sds((n, 4 * CHUNK), BF), sds((1, D), F32), sds((1, D), F32)],
        (k, v, q, pack_all, pack_all, own_seg, all_seg, cos, sin), 8 * n * total * D * 2,
        scratch=[pltpu.VMEM((32, total), F32), pltpu.VMEM((n, D), BF), pltpu.VMEM((n, D), BF)],
        scalars=(spot,), vmem=56,
    )


def input_back_kernel(pre_ref, dq_ref, dk_ref, dv_ref, wq_ref, wk_ref, wv_ref, out_ref):
    total = pre_ref[...]
    for d_ref, w_ref in ((dq_ref, wq_ref), (dk_ref, wk_ref), (dv_ref, wv_ref)):
        total = total + dot_nt(d_ref[...], w_ref[...])
    out_ref[...] = total.astype(out_ref.dtype)


def input_back(pre_one, dq, dk, dv, layer, wq, wk, wv, dtype):
    n = pre_one.shape[0]
    block = 256
    col = pl.BlockSpec((n, block), lambda j: (0, j))
    fixed = pl.BlockSpec((n, D), lambda j: (0, 0))
    weight = pl.BlockSpec((None, block, D), lambda j: (layer, j, 0))
    return call(
        input_back_kernel, "input_back", (D // block,), [col, fixed, fixed, fixed, weight, weight, weight],
        col, sds((n, D), dtype), (pre_one, dq, dk, dv, wq, wk, wv), 6 * n * D * D,
    )


def turned(ref, *parts):
    n = parts[0].shape[0]
    for i, part in enumerate(parts):
        ref[:, i * n : (i + 1) * n] = part.T


def shard_rows(ref, x):
    width = D // 8
    return jnp.concatenate(
        [ref[pl.ds(pl.multiple_of((2 * z + x) * width, 32), width), :] for z in range(4)], axis=0
    )


def inner_kernel(place_ref, a_ref, b_ref, gk_ref, gg_ref, keep_ref, send_ref, at_ref):
    @pl.when(pl.program_id(0) == 0)
    def _():
        turned(at_ref, a_ref[...], b_ref[...])

    g = jnp.concatenate([gk_ref[...], gg_ref[...]], axis=0)
    x = place_ref[0]
    for o_ref, side in ((keep_ref, x), (send_ref, 1 - x)):
        o_ref[...] = dot(shard_rows(at_ref, side), g).astype(BF).reshape(o_ref.shape)


def inner_pieces(spot, own, other, keep, got):
    n = own.shape[0]
    a = pl.BlockSpec((n, D), lambda y, s: (0, 0))
    g = pl.BlockSpec((n, FB), lambda y, s: (0, y))
    o = pl.BlockSpec((1, 4, D // 8, FB), lambda y, s: (y, 0, 0, 0))
    return call(
        inner_kernel, "inner_pieces", (2,), [a, a, g, g], [o, o], [sds((2, 4, D // 8, FB), BF)] * 2,
        (own, other, keep, got), 2 * 2 * n * D * 2 * FB,
        scratch=[pltpu.VMEM((D, 2 * n), BF)], scalars=(spot,),
    )


def outer_kernel(place_ref, a_ref, b_ref, gk_ref, gg_ref, keep_ref, send_ref, gt_ref):
    @pl.when(pl.program_id(0) == 0)
    def _():
        for h in range(2):
            part = slice(h * CHUNK, (h + 1) * CHUNK)
            turned(gt_ref.at[h], gk_ref[:, part], gg_ref[:, part])

    a = jnp.concatenate([a_ref[...], b_ref[...]], axis=0)
    y = place_ref[1]
    width = FF // 8
    for o_ref, side in ((keep_ref, y), (send_ref, 1 - y)):
        out = dot(gt_ref[side], a).astype(BF)
        for x in range(2):
            o_ref[0, x] = out[:, x * width : (x + 1) * width]


def outer_pieces(spot, own, other, keep, got):
    n = own.shape[0]
    a = pl.BlockSpec((n, 2 * FF // 8), lambda z, s: (0, 2 + z))
    g = pl.BlockSpec((n, 2 * CHUNK), lambda z, s: (0, 0))
    o = pl.BlockSpec((1, 2, CHUNK, FF // 8), lambda z, s: (z, 0, 0, 0))
    return call(
        outer_kernel, "outer_pieces", (4,), [a, a, g, g], [o, o], [sds((4, 2, CHUNK, FF // 8), BF)] * 2,
        (own, other, keep, got), 2 * 2 * n * FF * 2 * CHUNK,
        scratch=[pltpu.VMEM((2, CHUNK, 2 * n), BF)], scalars=(spot,),
    )


def query_out_kernel(place_ref, rows_ref, a_ref, b_ref, qk_ref, qg_ref, ok_ref, og_ref, keep_ref, send_ref, in_ref, at_ref):
    turned(in_ref, rows_ref[...])
    turned(at_ref, a_ref[...], b_ref[...])
    gq = jnp.concatenate([qk_ref[...], qg_ref[...]], axis=0)
    go = jnp.concatenate([ok_ref[...], og_ref[...]], axis=0)
    x = place_ref[0]
    for o_ref, side in ((keep_ref, x), (send_ref, 1 - x)):
        q = dot(shard_rows(in_ref, side), gq)
        o = dot(shard_rows(at_ref, side), go)
        for y in range(2):
            part = slice(y * CHUNK, (y + 1) * CHUNK)
            both = jnp.concatenate([q[:, part], o[:, part]], axis=1).astype(BF)
            o_ref[y] = both.reshape(o_ref.shape[1:])


def query_out_pieces(spot, rows, own, other, q_keep, q_got, keep, got):
    n = own.shape[0]
    a = pl.BlockSpec((n, D), lambda i, s: (0, 1))
    q = pl.BlockSpec((n, 2 * CHUNK), lambda i, s: (0, 0))
    g = pl.BlockSpec((n, 2 * CHUNK), lambda i, s: (0, 1))
    o = pl.BlockSpec((2, 4, D // 8, 2 * CHUNK), lambda i, s: (0, 0, 0, 0))
    return call(
        query_out_kernel, "query_out_pieces", (1,),
        [pl.BlockSpec((2 * n, D), lambda i, s: (0, 0)), a, a, q, q, g, g], [o, o],
        [sds((2, 4, D // 8, 2 * CHUNK), BF)] * 2, (rows, own, other, q_keep, q_got, keep, got),
        4 * 2 * n * D * 2 * CHUNK, scratch=[pltpu.VMEM((D, 2 * n), BF)] * 2, scalars=(spot,),
    )


def key_value_kernel(place_ref, rows_ref, gk_ref, gg_ref, keep_ref, send_ref, in_ref):
    turned(in_ref, rows_ref[...])
    x = place_ref[0]
    for y in range(2):
        part = slice(y * 2 * CHUNK, (y + 1) * 2 * CHUNK)
        g = jnp.concatenate([gk_ref[:, part], gg_ref[:, part]], axis=0)
        for o_ref, side in ((keep_ref, x), (send_ref, 1 - x)):
            o_ref[y] = dot(shard_rows(in_ref, side), g).astype(BF).reshape(o_ref.shape[1:])


def key_value_pieces(spot, rows, keep, got):
    n = keep.shape[0]
    g = pl.BlockSpec((n, 4 * CHUNK), lambda i, s: (0, 0))
    o = pl.BlockSpec((2, 4, D // 8, 2 * CHUNK), lambda i, s: (0, 0, 0, 0))
    return call(
        key_value_kernel, "key_value_pieces", (1,),
        [pl.BlockSpec((2 * n, D), lambda i, s: (0, 0)), g, g], [o, o], [sds((2, 4, D // 8, 2 * CHUNK), BF)] * 2,
        (rows, keep, got), 4 * 2 * n * D * 2 * CHUNK, scratch=[pltpu.VMEM((D, 2 * n), BF)], scalars=(spot,),
    )


def linear(z, x, y, c):
    return (z * 2 + x) * 4 + y * 2 + c


PLACES = [(z, x, y, c) for z in range(4) for x in range(2) for y in range(2) for c in range(2)]


def move(array, where):
    pairs = [(linear(*place), linear(*where(*place))) for place in PLACES]
    return lax.ppermute(array, BOTH, pairs)


def to_plane(z, x, y, c):
    return (2 * y + c, x, z >> 1, z & 1)


def other_core(z, x, y, c):
    return (z, x, y, 1 - c)


def other_x(z, x, y, c):
    return (z, 1 - x, y, c)


def other_y(z, x, y, c):
    return (z, x, 1 - y, c)


def other_xy(z, x, y, c):
    return (z, 1 - x, 1 - y, c)


def along_z(step):
    return lambda z, x, y, c: ((z + step) % 4, x, y, c)


def pick(array, index, axis):
    return lax.dynamic_index_in_dim(array, index, axis, keepdims=False)


def add(a, b):
    return (a.astype(F32) + b.astype(F32)).astype(BF)


class Small:
    def __init__(self):
        seq, rows = lax.axis_index("seq"), lax.axis_index("rows")
        self.z, self.x, self.y, self.c = seq // 2, seq % 2, rows // 2, rows % 2
        self.spot = jnp.stack([self.x, self.y, self.c, self.z]).astype(jnp.int32)

    def enter(self, array):
        return move(array, to_plane)

    leave = enter

    def starts(self, count):
        out = []
        for dc in (0, 1):
            for dx, dy in ((0, 0), (1, 0), (0, 1), (1, 1)):
                x, y, c = self.x ^ dx, self.y ^ dy, self.c ^ dc
                out.append(((2 * y + c) * 2 + x) * count)
        out[1:5] = [out[4], out[1], out[2], out[3]]
        return jnp.stack(out)

    def gather(self, array):
        near = [array, move(array, other_core)]
        far = jnp.concatenate([move(array, other_x), move(array, other_y), move(array, other_xy)], axis=0)
        return jnp.concatenate(near + [far, move(far, other_core)], axis=0)

    def finish(self, t):
        total = pick(t, self.z, 0).astype(F32)
        for k in (1, 2, 3):
            total = total + move(pick(t, (self.z + k) % 4, 0), along_z(k)).astype(F32)
        return total

    def x_first(self, keep, send):
        s = add(keep, move(send, other_x))
        return self.finish(add(pick(s, self.y, 0), move(pick(s, 1 - self.y, 0), other_y)))

    def y_first(self, keep, send):
        s = add(keep, move(send, other_y))
        return self.finish(add(pick(s, self.x, 1), move(pick(s, 1 - self.x, 1), other_x)))

    def carry(self, kept):
        kept["pack_other"] = move(kept["pack"], other_core)

    def feed_grads(self, kept, keep, send, keep_in, send_in):
        got, got_in = move(send, other_core), move(send_in, other_core)
        own, other = kept["pack"], kept["pack_other"]
        inner = self.x_first(*inner_pieces(self.spot, own, other, keep_in, got_in))
        outer = self.y_first(*outer_pieces(self.spot, own, other, keep, got))
        return {"inner": inner, "outer": outer.T, "keep": keep, "got": got}

    def query_grads(self, kept, grads, dq, keep, send):
        got = move(send, other_core)
        pieces = query_out_pieces(
            self.spot, kept["rows"], kept["pack"], kept["pack_other"], keep, got, grads["keep"], grads["got"]
        )
        both = self.x_first(*pieces)
        grads["query"], grads["out"] = both[:, :CHUNK], both[:, CHUNK:]

    def key_grads(self, kept, grads, dk, dv, keep, send):
        got = move(send, other_core)
        both = self.x_first(*key_value_pieces(self.spot, kept["rows"], keep, got))
        grads["key"], grads["value"] = both[:, :CHUNK], both[:, CHUNK:]

    def vectors(self, flat):
        for where in (other_core, other_x, other_y):
            flat = flat + move(flat, where)
        flat = flat + move(flat, lambda z, x, y, c: (z ^ 1, x, y, c))
        return flat + move(flat, lambda z, x, y, c: (z ^ 2, x, y, c))


class Large:
    def __init__(self):
        self.shards = lax.axis_size("seq")
        self.spot = jnp.zeros((4,), jnp.int32)

    def enter(self, array):
        return array

    leave = enter

    def starts(self, count):
        me = lax.axis_index("seq")
        return (me + jnp.arange(self.shards, dtype=jnp.int32)) % self.shards * count

    def gather(self, array):
        whole_row = lax.all_gather(array, "seq", axis=0, tiled=True)
        return jnp.roll(whole_row, -lax.axis_index("seq") * array.shape[0], axis=0)

    def carry(self, kept):
        pass

    def spread(self, left, right):
        grad = lax.dot_general(left, right, (((0,), (0,)), ((), ())), preferred_element_type=F32).astype(BF)
        grad = lax.psum_scatter(grad, "seq", scatter_dimension=0, tiled=True)
        return lax.psum_scatter(grad, "rows", scatter_dimension=1, tiled=True).astype(F32)

    def feed_grads(self, kept, keep, send, keep_in, send_in):
        def mixed(a, b, at, w):
            return jnp.concatenate([a[:, at : at + w], b[:, at : at + w], a[:, at + w : at + 2 * w], b[:, at + w : at + 2 * w]], axis=1)

        pack = kept["pack"]
        return {
            "inner": self.spread(pack[:, :D], mixed(keep_in, send_in, 0, FB)),
            "outer": self.spread(pack[:, 2 * D :], mixed(keep, send, 0, CHUNK)),
            "out": self.spread(pack[:, D : 2 * D], mixed(keep, send, 2 * CHUNK, CHUNK)),
        }

    def query_grads(self, kept, grads, dq, keep, send):
        grads["query"] = self.spread(kept["rows"][: dq.shape[0]], dq)

    def key_grads(self, kept, grads, dk, dv, keep, send):
        grads["key"] = self.spread(kept["rows"][: dk.shape[0]], dk)
        grads["value"] = self.spread(kept["rows"][: dk.shape[0]], dv)

    def vectors(self, flat):
        return lax.psum(flat, BOTH)


def doc_layout(lengths_row, index):
    ends = jnp.cumsum(lengths_row, dtype=jnp.int32)
    passed = (index[:, None] >= ends[None, :]).astype(jnp.int32)
    segment = jnp.sum(passed, axis=1, dtype=jnp.int32)
    begin = jnp.sum(passed * lengths_row[None, :], axis=1, dtype=jnp.int32)
    return (segment, (index - begin).astype(jnp.int32))


def rotary_tables(position):
    lane = jnp.arange(LANES, dtype=jnp.int32)
    pairs = (lane % HEAD_DIM // 2).astype(F32)
    inverse = jnp.power(jnp.float32(10000.0), -2.0 * pairs / HEAD_DIM)
    angle = position.astype(F32)[:, None] * inverse[None, :]
    return jnp.cos(angle), jnp.sin(angle) * jnp.where(lane % 2 == 0, -1.0, 1.0)[None, :]


def body(large, tokens, lengths, cotangent, *params):
    wq, bq, wk, bk, wv, bv, wo, bo, g1, c1, wi, bi, wu, bu, g2, c2 = params
    place = Large() if large else Small()
    spot = place.spot
    n = tokens.shape[1]
    current = place.enter(tokens[0])
    lengths_row = place.enter(lengths)[0]
    vec = jnp.stack([bq, bk, bv, bo, g1, c1, bu, g2, c2], axis=1).astype(F32)
    bi = bi.astype(F32)[:, None, :]
    index = (place.starts(n)[:, None] + jnp.arange(n, dtype=jnp.int32)).reshape(-1)
    segment, position = doc_layout(lengths_row, index)
    own_seg, all_seg = segment[:n, None], segment[None, :]
    cos, sin = rotary_tables(position)
    saved = []
    current_b = current
    for layer in range(LAYERS):
        rows = place.gather(current_b)
        q, k, v = project(rows, layer, wq, wk, wv, vec, cos, sin)
        attn, lse = attend(q, k, v, own_seg, all_seg, n)
        current, current_b, n1, n2, stat, slope, pack = feed_forward(current, attn, layer, wo, wi, bi, wu, vec)
        kept = dict(rows=rows, q=q, k=k, v=v, attn=attn, lse=lse, n1=n1, n2=n2, stat=stat, slope=slope, pack=pack)
        place.carry(kept)
        saved.append(kept)
    output = place.leave(current_b)
    grad = place.enter(cotangent[0])
    grads, sums = [None] * LAYERS, [None] * LAYERS
    for layer in range(LAYERS - 1, -1, -1):
        kept = saved[layer]
        keep, send, keep_in, send_in, pre_one, pack, delta, feed_sums, inner_sum = feed_forward_back(
            spot, grad, kept, layer, wu, wi, wo, vec
        )
        pack_all = place.gather(pack)
        found = place.feed_grads(kept, keep, send, keep_in, send_in)
        dq, q_keep, q_send, dq_sum = query_back(
            spot, kept["q"], kept["k"], kept["v"], pack, kept["lse"], delta, own_seg, all_seg, cos, sin
        )
        place.query_grads(kept, found, dq, q_keep, q_send)
        dk, dv, kv_keep, kv_send, dk_sum, dv_sum = key_back(
            spot, kept["k"], kept["v"], kept["q"], pack_all, own_seg, all_seg, cos, sin, n
        )
        place.key_grads(kept, found, dk, dv, kv_keep, kv_send)
        grad = input_back(pre_one, dq, dk, dv, layer, wq, wk, wv, F32 if layer else BF)
        grads[layer] = found
        shards = lax.axis_size("seq")
        sums[layer] = jnp.concatenate(
            [
                jnp.concatenate([feed_sums[:6], dq_sum, dk_sum, dv_sum], axis=0).reshape(9, shards, -1).swapaxes(0, 1),
                inner_sum.reshape(shards, FF // D, -1),
            ],
            axis=1,
        )
    tokens_grad = place.leave(grad)
    flat = place.vectors(jnp.stack(sums, axis=1).reshape(shards, -1))
    flat = pick(flat, lax.axis_index("seq"), 0).reshape(LAYERS, 13, -1)
    g2_, c2_, bu_, g1_, c1_, bo_, bq_, bk_, bv_ = [flat[:, i] for i in range(9)]
    bi_ = flat[:, 9:].reshape(LAYERS, -1)
    m = {name: jnp.stack([grads[layer][name] for layer in range(LAYERS)]) for name in grads[0] if name not in ("keep", "got")}
    return (
        output[None], tokens_grad[None],
        m["query"], bq_, m["key"], bk_, m["value"], bv_, m["out"], bo_, g1_, c1_,
        m["inner"], bi_, m["outer"], bu_, g2_, c2_,
    )


def solution(mesh):
    token = P("rows", "seq", None)
    mat, vec = P(None, "seq", "rows"), P(None, "seq")
    small = (mesh.shape["seq"], mesh.shape["rows"]) == (8, 4)
    return jax.shard_map(
        functools.partial(body, not small),
        mesh=mesh,
        in_specs=(token, P("rows", None), token) + (P(),) * 16,
        out_specs=(token, token, mat, vec, mat, vec, mat, vec, mat, vec, vec, vec, mat, vec, mat, vec, vec, vec),
        check_vma=False,
    )
```

time: 2330 us -> 472 us (0.20)
  blocking collectives: 806 us -> 0 us
  waiting for transfers between devices: 922 us -> 127 us
  local copies, waits for them, and re-layouts: 343 us -> 92.8 us
  matrix products: 147 us -> 0 us
  Pallas kernels: 0 us -> 119 us
  starting transfers between devices: 1.95 us -> 96.8 us
  other arithmetic: 79.8 us -> 30.6 us
    unnamed x42 -> x0, waiting for transfers between devices: 691 us -> none
    unnamed x1 -> x0, blocking collectives: 666 us -> none
    unnamed x364 -> x274, local copies, waits for them, and re-layouts: 264 us -> 69.9 us
    all_gather x8 -> x0, waiting for transfers between devices: 158 us -> none  [the longest x2 80.5 us: layer_forward(): keys_piece = lax.all_gather(key_b, 'seq', axis=0, tiled=True)]
    dot_general x48 -> x0, matrix products: 147 us -> none  [the longest x12 31 us: project(): jnp.dot(inputs_b, weight, preferred_element_type=jnp.float32)]
    all_gather x4 -> x0, blocking collectives: 129 us -> none  [the longest x2 64.9 us: layer_backward(): lax.all_gather(log_total.T, 'seq', axis=0, tiled=True)]
    ppermute x0 -> x80, waiting for transfers between devices: none -> 127 us  [move(): return lax.ppermute(array, BOTH, pairs)]
    pallas_call x0 -> x22, Pallas kernels: none -> 119 us  [call(): pl.pallas_call(kernel, name=name, grid_spec=pltpu.PrefetchScalarGridSpec(...]
  transfers between devices with their start and end apart: 27 -> 80, of which waited for: 21 -> 26; matrix products, arithmetic and copies ran while one was open for 22% -> 15% of each run, Pallas kernels for 0% -> 19%
where the time goes in v1:
time: 472 us; the launch traced here: 468 us
  waiting for transfers between devices  127 us (27%)
  Pallas kernels  119 us (25%)
  starting transfers between devices  96.8 us (21%)
  local copies, waits for them, and re-layouts  92.8 us (20%)
  other arithmetic  30.6 us (6%)
    ppermute x80, waiting for transfers between devices, move(): return lax.ppermute(array, BOTH, pairs)  127 us
    pallas_call x22, Pallas kernels, call(): pl.pallas_call(kernel, name=name, grid_spec=pltpu.PrefetchScalarGridSpec(...  119 us
    ppermute x80, starting transfers between devices, move(): return lax.ppermute(array, BOTH, pairs)  96.8 us
    unnamed x274, local copies, waits for them, and re-layouts  69.9 us
    convert_element_type x16, other arithmetic, add(): return (a.astype(F32) + b.astype(F32)).astype(BF)  12.4 us
  transfers between devices with their start and end apart: 80, of which 26 were waited for; matrix products, arithmetic and copies ran while one was open for 15% of the time, Pallas kernels for 19%

profile of v1, /device:TPU:0, one launch (start us, length us, event | category | flops | bytes accessed | tf_op | source)
XLA Modules:
  0.0 468.0 jit_solution(17852101475636230983)
XLA Ops:
  16.2 4.9 %collective-permute-start.3 = (bf16[128,768]{1,0:T(8,128)(2,1)}, bf16[128,768]{1,0:T(8,128)(2,1)S(1)}, u32[]{:S(2)}, u32[]{:S(2)}) collective-permute-start(bf16[128,768]{1,0:T(8,128)(2,1)} %collective-permute-done.x_ref), channel_id=1, source_target_pairs={{0,2},{1,3},{2,0},{3,1},{4,6},{5,7},{6,4},{7,5},{8,10},{9,11},{10,... | collective-permute-start | bytes 589832 | tf_op jit(solution)/shard_map/ppermute | solution.py:630
  23.1 7.0 %collective-permute-done.3 = bf16[128,768]{1,0:T(8,128)(2,1)S(1)} collective-permute-done((bf16[128,768]{1,0:T(8,128)(2,1)}, bf16[128,768]{1,0:T(8,128)(2,1)S(1)}, u32[]{:S(2)}, u32[]{:S(2)}) %collective-permute-start.3) | collective-permute-done | bytes 196640 | tf_op jit(solution)/shard_map/ppermute | solution.py:630
  49.9 6.9 %attend.2 = (f32[128,768]{1,0:T(8,128)}, f32[128,128]{1,0:T(8,128)}) custom-call(bf16[1024,768]{1,0:T(8,128)(2,1)} %copy-done.1, bf16[1024,768]{1,0:T(8,128)(2,1)} %copy-done.2, bf16[1024,768]{1,0:T(8,128)(2,1)} %copy-done.3, s32[128,1]{1,0:T(8,128)} %copy.75.own_ref, s32[1,1024]{1,0:T(1,128)} %bitcast.200), custom_call_target="tpu_custom_call" | custom-call | flops 805306368 | bytes 5181952 | tf_op jit(solution)/shard_map/attend/pallas_call | solution.py:42
  57.8 7.5 %ffn.2 = (f32[128,768]{1,0:T(8,128)S(1)}, bf16[128,768]{1,0:T(8,128)(2,1)}, f32[128,768]{1,0:T(8,128)S(1)}, f32[128,768]{1,0:T(8,128)S(1)}, f32[128,128]{1,0:T(8...) custom-call(bf16[128,768]{1,0:T(8,128)(2,1)} %collective-permute-done.x_ref, ...), custom_call_target="tpu_custom_call" | custom-call | flops 1358954496 | bytes 26097664 | tf_op jit(solution)/shard_map/ffn/pallas_call | solution.py:42
  100.9 6.8 %attend.3 = (f32[128,768]{1,0:T(8,128)}, f32[128,128]{1,0:T(8,128)}) custom-call(bf16[1024,768]{1,0:T(8,128)(2,1)} %copy-done.4, bf16[1024,768]{1,0:T(8,128)(2,1)} %copy-done.5, bf16[1024,768]{1,0:T(8,128)(2,1)} %copy-done.6, s32[128,1]{1,0:T(8,128)} %copy.75.own_ref, s32[1,1024]{1,0:T(1,128)} %bitcast.201), custom_call_target="tpu_custom_call" | custom-call | flops 805306368 | bytes 5181952 | tf_op jit(solution)/shard_map/attend/pallas_call | solution.py:42
  108.8 7.2 %ffn.3 = (f32[128,768]{1,0:T(8,128)}, bf16[128,768]{1,0:T(8,128)(2,1)S(1)}, f32[128,768]{1,0:T(8,128)S(1)}, f32[128,768]{1,0:T(8,128)S(1)}, f32[128,128]{1,0:T(8...) custom-call(f32[128,768]{1,0:T(8,128)S(1)} %copy-done.68, f32[128,768]{1,0:T(8,128)S(1)} %copy-done.38, ...), custom_call_target="tpu_custom_call" | custom-call | flops 1358954496 | bytes 26294272 | tf_op jit(solution)/shard_map/ffn/pallas_call | solution.py:42
  117.7 10.0 %ffn_back.2 = (bf16[128,768]{1,0:T(8,128)(2,1)S(1)}, bf16[128,768]{1,0:T(8,128)(2,1)S(1)}, bf16[128,1536]{1,0:T(8,128)(2,1)S(1)}, bf16[128,1536]{1,0:T(8,128)(2,...) custom-call(s32[4]{0:T(128)S(1)} %pad_add_fusion.place_ref, ...), custom_call_target="tpu_custom_call" | custom-call | flops 1358954496 | bytes 26273792 | tf_op jit(solution)/shard_map/ffn_back/pallas_call | solution.py:42
  143.0 5.5 %collective-permute-done.16 = bf16[128,896]{1,0:T(8,128)(2,1)} collective-permute-done((bf16[128,896]{1,0:T(8,128)(2,1)}, bf16[128,896]{1,0:T(8,128)(2,1)}, u32[]{:S(2)}, u32[]{:S(2)}) %collective-permute-start.16) | collective-permute-done | bytes 229408 | tf_op jit(solution)/shard_map/ppermute | solution.py:630
  150.3 7.9 %query_back.2 = (bf16[128,768]{1,0:T(8,128)(2,1)}, bf16[128,384]{1,0:T(8,128)(2,1)}, bf16[128,384]{1,0:T(8,128)(2,1)}, f32[1,768]{1,0:T(1,128)}) custom-call(s32[4]{0:T(128)} %copy-done.80, bf16[1024,768]{1,0:T(8,128)(2,1)} %copy-done.4, bf16[1024,768]{1,0:T(8,128)(2,1)} %copy-done.5, bf16[1024,768]{1,0:T(8,128)(2,1)} %copy-done.6, ...), custom_call_target="tpu_custom_call" | custom-call | flops 1207959552 | bytes 6528512 | tf_op jit(solution)/shard_map/query_back/pallas_call | solution.py:42
  167.4 9.2 %key_back.2 = (bf16[128,768]{1,0:T(8,128)(2,1)}, bf16[128,768]{1,0:T(8,128)(2,1)}, bf16[128,768]{1,0:T(8,128)(2,1)}, bf16[128,768]{1,0:T(8,128)(2,1)}, f32[1,768]{1,0:T(1,128)}, /*index=5*/f32[1,768]{1,0:T(1,128)}) custom-call(s32[4]{0:T(128)} %copy-done.80, bf16[1024,768]{1,0:T(8,128)(2,1)} %copy-done.5, bf16[1024,768]{1,0:T(8,128)(2,1)} %copy-done.6, ...), custom_call_target="tpu_custom_call" | custom-call | flops 1610612736 | bytes 10234368 | tf_op jit(solution)/shard_map/key_back/pallas_call | solution.py:42
  184.0 10.0 %ffn_back.3 = (bf16[128,768]{1,0:T(8,128)(2,1)S(1)}, bf16[128,768]{1,0:T(8,128)(2,1)}, bf16[128,1536]{1,0:T(8,128)(2,1)S(1)}, bf16[128,1536]{1,0:T(8,128)(2,1)S(...) custom-call(s32[4]{0:T(128)S(1)} %copy-done.81, ...), custom_call_target="tpu_custom_call" | custom-call | flops 1358954496 | bytes 26470400 | tf_op jit(solution)/shard_map/ffn_back/pallas_call | solution.py:42
  198.2 8.0 %query_back.3 = (bf16[128,768]{1,0:T(8,128)(2,1)}, bf16[128,384]{1,0:T(8,128)(2,1)}, bf16[128,384]{1,0:T(8,128)(2,1)}, f32[1,768]{1,0:T(1,128)}) custom-call(s32[4]{0:T(128)} %copy-done.80, bf16[1024,768]{1,0:T(8,128)(2,1)} %copy-done.1, bf16[1024,768]{1,0:T(8,128)(2,1)} %copy-done.2, bf16[1024,768]{1,0:T(8,128)(2,1)} %copy-done.3, ...), custom_call_target="tpu_custom_call" | custom-call | flops 1207959552 | bytes 6528512 | tf_op jit(solution)/shard_map/query_back/pallas_call | solution.py:42
  230.1 5.4 %collective-permute-done.21 = bf16[128,896]{1,0:T(8,128)(2,1)S(1)} collective-permute-done((bf16[128,896]{1,0:T(8,128)(2,1)}, bf16[128,896]{1,0:T(8,128)(2,1)S(1)}, u32[]{:S(2)}, u32[]{:S(2)}) %collective-permute-start.21) | collective-permute-done | bytes 229408 | tf_op jit(solution)/shard_map/ppermute | solution.py:630
  264.5 8.8 %key_back.3 = (bf16[128,768]{1,0:T(8,128)(2,1)}, bf16[128,768]{1,0:T(8,128)(2,1)}, bf16[128,768]{1,0:T(8,128)(2,1)}, bf16[128,768]{1,0:T(8,128)(2,1)}, f32[1,768]{1,0:T(1,128)}, /*index=5*/f32[1,768]{1,0:T(1,128)}) custom-call(s32[4]{0:T(128)} %copy-done.80, bf16[1024,768]{1,0:T(8,128)(2,1)} %copy-done.2, bf16[1024,768]{1,0:T(8,128)(2,1)} %copy-done.3, ...), custom_call_target="tpu_custom_call" | custom-call | flops 1610612736 | bytes 10234368 | tf_op jit(solution)/shard_map/key_back/pallas_call | solution.py:42
  298.0 5.7 %collective-permute-start.32 = (bf16[96,384]{1,0:T(8,128)(2,1)S(1)}, bf16[96,384]{1,0:T(8,128)(2,1)S(1)}, u32[]{:S(2)}, u32[]{:S(2)}) collective-permute-start(bf16[96,384]{1,0:T(8,128)(2,1)S(1)} %get-tuple-element.193), channel_id=1, source_target_pairs={{0,24},{1,25},{2,26},{3,27},{4,28},{5,29},{6,30},{7,31},{8,0},{9,1... | collective-permute-start | bytes 221192 | tf_op jit(solution)/shard_map/ppermute | solution.py:630
  344.3 6.5 %collective-permute-done.65 = bf16[2,4,96,768]{3,2,1,0:T(8,128)(2,1)} collective-permute-done((bf16[2,4,96,768]{3,2,1,0:T(8,128)(2,1)}, bf16[2,4,96,768]{3,2,1,0:T(8,128)(2,1)}, u32[]{:S(2)}, u32[]{:S(2)}) %collective-permute-start.65) | collective-permute-done | bytes 1179680 | tf_op jit(solution)/shard_map/ppermute | solution.py:630
  355.7 20.5 %collective-permute-done.59 = bf16[2,4,96,768]{3,2,1,0:T(8,128)(2,1)} collective-permute-done((bf16[2,4,96,768]{3,2,1,0:T(8,128)(2,1)}, bf16[2,4,96,768]{3,2,1,0:T(8,128)(2,1)}, u32[]{:S(2)}, u32[]{:S(2)}) %collective-permute-start.59) | collective-permute-done | bytes 1179680 | tf_op jit(solution)/shard_map/ppermute | solution.py:630
  378.7 10.1 %collective-permute-done.47 = bf16[2,4,96,384]{3,2,1,0:T(8,128)(2,1)} collective-permute-done((bf16[2,4,96,384]{3,2,1,0:T(8,128)(2,1)S(1)}, bf16[2,4,96,384]{3,2,1,0:T(8,128)(2,1)}, u32[]{:S(2)}, u32[]{:S(2)}) %collective-permute-start.47) | collective-permute-done | bytes 589856 | tf_op jit(solution)/shard_map/ppermute | solution.py:630
  391.0 10.3 %collective-permute-done.71 = bf16[4,192,384]{2,1,0:T(8,128)(2,1)S(1)} collective-permute-done((bf16[4,192,384]{2,1,0:T(8,128)(2,1)S(1)}, bf16[4,192,384]{2,1,0:T(8,128)(2,1)S(1)}, u32[]{:S(2)}, u32[]{:S(2)}) %collective-permute-start.71) | collective-permute-done | bytes 589856 | tf_op jit(solution)/shard_map/ppermute | solution.py:630
  405.7 6.7 %collective-permute-done.76 = bf16[4,192,384]{2,1,0:T(8,128)(2,1)S(1)} collective-permute-done((bf16[4,192,384]{2,1,0:T(8,128)(2,1)S(1)}, bf16[4,192,384]{2,1,0:T(8,128)(2,1)S(1)}, u32[]{:S(2)}, u32[]{:S(2)}) %collective-permute-start.76) | collective-permute-done | bytes 589856 | tf_op jit(solution)/shard_map/ppermute | solution.py:630
  423.2 5.9 %collective-permute-done.73 = bf16[192,384]{1,0:T(8,128)(2,1)S(1)} collective-permute-done((bf16[192,384]{1,0:T(8,128)(2,1)S(1)}, bf16[192,384]{1,0:T(8,128)(2,1)S(1)}, u32[]{:S(2)}, u32[]{:S(2)}) %collective-permute-start.73) | collective-permute-done | bytes 147488 | tf_op jit(solution)/shard_map/ppermute | solution.py:630
  438.0 8.8 %collective-permute-done.68 = bf16[96,768]{1,0:T(8,128)(2,1)S(1)} collective-permute-done((bf16[96,768]{1,0:T(8,128)(2,1)S(1)}, bf16[96,768]{1,0:T(8,128)(2,1)S(1)}, u32[]{:S(2)}, u32[]{:S(2)}) %collective-permute-start.68) | collective-permute-done | bytes 147488 | tf_op jit(solution)/shard_map/ppermute | solution.py:630
  450.6 9.0 %collective-permute-done.78 = bf16[192,384]{1,0:T(8,128)(2,1)S(1)} collective-permute-done((bf16[192,384]{1,0:T(8,128)(2,1)S(1)}, bf16[192,384]{1,0:T(8,128)(2,1)S(1)}, u32[]{:S(2)}, u32[]{:S(2)}) %collective-permute-start.78) | collective-permute-done | bytes 147488 | tf_op jit(solution)/shard_map/ppermute | solution.py:630
  460.5 5.2 %collective-permute-done.62 = bf16[96,768]{1,0:T(8,128)(2,1)S(1)} collective-permute-done((bf16[96,768]{1,0:T(8,128)(2,1)S(1)}, bf16[96,768]{1,0:T(8,128)(2,1)S(1)}, u32[]{:S(2)}, u32[]{:S(2)}) %collective-permute-start.62) | collective-permute-done | bytes 147488 | tf_op jit(solution)/shard_map/ppermute | solution.py:630
  (537 shorter events, 271.9 us)
Async XLA Ops:
  74.2 42.8 %collective-permute-start.13 = (bf16[128,768]{1,0:T(8,128)(2,1)}, bf16[128,768]{1,0:T(8,128)(2,1)}, u32[]{:S(2)}, u32[]{:S(2)}) collective-permute-start(bf16[128,768]{1,0:T(8,128)(2,1)} %bitcast.29), channel_id=1, source_target_pairs={{0,0},{1,8},{2,16},{3,24},{4,4},{5,12},{6,20},{7,28},{8,1},{9,9},{... | collective-permute-start | bytes 589832 | tf_op jit(solution)/shard_map/ppermute | solution.py:630
  137.3 71.4 %collective-permute-start.25 = (bf16[128,4608]{1,0:T(8,128)(2,1)S(1)}, bf16[128,4608]{1,0:T(8,128)(2,1)}, u32[]{:S(2)}, u32[]{:S(2)}) collective-permute-start(bf16[128,4608]{1,0:T(8,128)(2,1)S(1)} %copy-done.10), channel_id=1, source_target_pairs={{0,1},{1,0},{2,3},{3,2},{4,5},{5,4},{6,7},{7,6},{8,9},{9,8},{10,11... | collective-permute-start | bytes 3538952 | tf_op jit(solution)/shard_map/ppermute | solution.py:630
  137.3 22.5 %collective-permute-start.14 = (bf16[128,896]{1,0:T(8,128)(2,1)}, bf16[128,896]{1,0:T(8,128)(2,1)}, u32[]{:S(2)}, u32[]{:S(2)}) collective-permute-start(bf16[128,896]{1,0:T(8,128)(2,1)} %get-tuple-element.112.g_ref), channel_id=1, source_target_pairs={{0,1},{1,0},{2,3},{3,2},{4,5},{5,4},{6,7},{7,6},{8,9},{9,8},{10,11... | collective-permute-start | bytes 688136 | tf_op jit(solution)/shard_map/ppermute | solution.py:630
  148.5 89.5 %collective-permute-start.33 = (bf16[128,4608]{1,0:T(8,128)(2,1)}, bf16[128,4608]{1,0:T(8,128)(2,1)}, u32[]{:S(2)}, u32[]{:S(2)}) collective-permute-start(bf16[128,4608]{1,0:T(8,128)(2,1)} %copy-done.11), channel_id=1, source_target_pairs={{0,1},{1,0},{2,3},{3,2},{4,5},{5,4},{6,7},{7,6},{8,9},{9,8},{10,11... | collective-permute-start | bytes 3538952 | tf_op jit(solution)/shard_map/ppermute | solution.py:630
  198.2 28.5 %collective-permute-start.19 = (bf16[128,896]{1,0:T(8,128)(2,1)}, bf16[128,896]{1,0:T(8,128)(2,1)}, u32[]{:S(2)}, u32[]{:S(2)}) collective-permute-start(bf16[128,896]{1,0:T(8,128)(2,1)} %get-tuple-element.123.g_ref), channel_id=1, source_target_pairs={{0,1},{1,0},{2,3},{3,2},{4,5},{5,4},{6,7},{7,6},{8,9},{9,8},{10,11... | collective-permute-start | bytes 688136 | tf_op jit(solution)/shard_map/ppermute | solution.py:630
  228.9 28.2 %collective-permute-start.28 = (bf16[2,4,96,384]{3,2,1,0:T(8,128)(2,1)S(1)}, bf16[2,4,96,384]{3,2,1,0:T(8,128)(2,1)S(1)}, u32[]{:S(2)}, u32[]{:S(2)}) collective-permute-start(bf16[2,4,96,384]{3,2,1,0:T(8,128)(2,1)S(1)} %get-tuple-element.134), channel_id=1, source_target_pairs={{0,4},{1,5},{2,6},{3,7},{4,0},{5,1},{6,2},{7,3},{8,12},{9,13},{10,... | collective-permute-start | bytes 1769480 | tf_op jit(solution)/shard_map/ppermute | solution.py:630
  236.5 24.4 %collective-permute-start.53 = (bf16[2,4,96,384]{3,2,1,0:T(8,128)(2,1)S(1)}, bf16[2,4,96,384]{3,2,1,0:T(8,128)(2,1)S(1)}, u32[]{:S(2)}, u32[]{:S(2)}) collective-permute-start(bf16[2,4,96,384]{3,2,1,0:T(8,128)(2,1)S(1)} %get-tuple-element.159), channel_id=1, source_target_pairs={{0,4},{1,5},{2,6},{3,7},{4,0},{5,1},{6,2},{7,3},{8,12},{9,13},{10,... | collective-permute-start | bytes 1769480 | tf_op jit(solution)/shard_map/ppermute | solution.py:630
  238.0 104.5 %collective-permute-start.70 = (bf16[4,2,192,384]{3,2,0,1:T(8,128)(2,1)}, bf16[4,2,192,384]{3,2,0,1:T(8,128)(2,1)}, u32[]{:S(2)}, u32[]{:S(2)}) collective-permute-start(bf16[4,2,192,384]{3,2,0,1:T(8,128)(2,1)} %copy.84), channel_id=1, source_target_pairs={{0,2},{1,3},{2,0},{3,1},{4,6},{5,7},{6,4},{7,5},{8,10},{9,11},{10,... | collective-permute-start | bytes 3538952 | tf_op jit(solution)/shard_map/ppermute | solution.py:630
  252.6 24.9 %collective-permute-start.36 = (bf16[2,4,96,384]{3,2,1,0:T(8,128)(2,1)}, bf16[2,4,96,384]{3,2,1,0:T(8,128)(2,1)}, u32[]{:S(2)}, u32[]{:S(2)}) collective-permute-start(bf16[2,4,96,384]{3,2,1,0:T(8,128)(2,1)} %get-tuple-element.141), channel_id=1, source_target_pairs={{0,4},{1,5},{2,6},{3,7},{4,0},{5,1},{6,2},{7,3},{8,12},{9,13},{10,... | collective-permute-start | bytes 1769480 | tf_op jit(solution)/shard_map/ppermute | solution.py:630
  258.2 31.5 %collective-permute-start.29 = (bf16[4,96,384]{2,1,0:T(8,128)(2,1)}, bf16[4,96,384]{2,1,0:T(8,128)(2,1)}, u32[]{:S(2)}, u32[]{:S(2)}) collective-permute-start(bf16[4,96,384]{2,1,0:T(8,128)(2,1)} %dynamic-slice_bitcast_fusion.7), channel_id=1, source_target_pairs={{0,2},{1,3},{2,0},{3,1},{4,6},{5,7},{6,4},{7,5},{8,10},{9,11},{10,... | collective-permute-start | bytes 884744 | tf_op jit(solution)/shard_map/ppermute | solution.py:630
  261.8 31.1 %collective-permute-start.54 = (bf16[4,96,384]{2,1,0:T(8,128)(2,1)}, bf16[4,96,384]{2,1,0:T(8,128)(2,1)}, u32[]{:S(2)}, u32[]{:S(2)}) collective-permute-start(bf16[4,96,384]{2,1,0:T(8,128)(2,1)} %dynamic-slice_bitcast_fusion.4), channel_id=1, source_target_pairs={{0,2},{1,3},{2,0},{3,1},{4,6},{5,7},{6,4},{7,5},{8,10},{9,11},{10,... | collective-permute-start | bytes 884744 | tf_op jit(solution)/shard_map/ppermute | solution.py:630
  281.5 23.5 %collective-permute-start.37 = (bf16[4,96,384]{2,1,0:T(8,128)(2,1)S(1)}, bf16[4,96,384]{2,1,0:T(8,128)(2,1)S(1)}, u32[]{:S(2)}, u32[]{:S(2)}) collective-permute-start(bf16[4,96,384]{2,1,0:T(8,128)(2,1)S(1)} %dynamic-slice_bitcast_fusion.6), channel_id=1, source_target_pairs={{0,2},{1,3},{2,0},{3,1},{4,6},{5,7},{6,4},{7,5},{8,10},{9,11},{10,... | collective-permute-start | bytes 884744 | tf_op jit(solution)/shard_map/ppermute | solution.py:630
  292.9 28.7 %collective-permute-start.43 = (f32[8,2496]{1,0:T(8,128)S(1)}, f32[8,2496]{1,0:T(8,128)S(1)}, u32[]{:S(2)}, u32[]{:S(2)}) collective-permute-start(f32[8,2496]{1,0:T(8,128)S(1)} %add.410), channel_id=1, source_target_pairs={{0,2},{1,3},{2,0},{3,1},{4,6},{5,7},{6,4},{7,5},{8,10},{9,11},{10,... | collective-permute-start | bytes 239624 | tf_op jit(solution)/shard_map/ppermute | solution.py:630
  321.6 29.2 %collective-permute-start.65 = (bf16[2,4,96,768]{3,2,1,0:T(8,128)(2,1)}, bf16[2,4,96,768]{3,2,1,0:T(8,128)(2,1)}, u32[]{:S(2)}, u32[]{:S(2)}) collective-permute-start(bf16[2,4,96,768]{3,2,1,0:T(8,128)(2,1)} %get-tuple-element.167), channel_id=1, source_target_pairs={{0,4},{1,5},{2,6},{3,7},{4,0},{5,1},{6,2},{7,3},{8,12},{9,13},{10,... | collective-permute-start | bytes 3538952 | tf_op jit(solution)/shard_map/ppermute | solution.py:630
  322.0 31.5 %collective-permute-start.75 = (bf16[4,2,192,384]{3,2,1,0:T(8,128)(2,1)S(1)}, bf16[4,2,192,384]{3,2,1,0:T(8,128)(2,1)}, u32[]{:S(2)}, u32[]{:S(2)}) collective-permute-start(bf16[4,2,192,384]{3,2,1,0:T(8,128)(2,1)S(1)} %copy-done.95), channel_id=1, source_target_pairs={{0,2},{1,3},{2,0},{3,1},{4,6},{5,7},{6,4},{7,5},{8,10},{9,11},{10,... | collective-permute-start | bytes 3538952 | tf_op jit(solution)/shard_map/ppermute | solution.py:630
  325.9 50.3 %collective-permute-start.59 = (bf16[2,4,96,768]{3,2,1,0:T(8,128)(2,1)}, bf16[2,4,96,768]{3,2,1,0:T(8,128)(2,1)}, u32[]{:S(2)}, u32[]{:S(2)}) collective-permute-start(bf16[2,4,96,768]{3,2,1,0:T(8,128)(2,1)} %get-tuple-element.163), channel_id=1, source_target_pairs={{0,4},{1,5},{2,6},{3,7},{4,0},{5,1},{6,2},{7,3},{8,12},{9,13},{10,... | collective-permute-start | bytes 3538952 | tf_op jit(solution)/shard_map/ppermute | solution.py:630
  336.1 52.7 %collective-permute-start.47 = (bf16[2,4,96,384]{3,2,1,0:T(8,128)(2,1)S(1)}, bf16[2,4,96,384]{3,2,1,0:T(8,128)(2,1)}, u32[]{:S(2)}, u32[]{:S(2)}) collective-permute-start(bf16[2,4,96,384]{3,2,1,0:T(8,128)(2,1)S(1)} %get-tuple-element.155), channel_id=1, source_target_pairs={{0,4},{1,5},{2,6},{3,7},{4,0},{5,1},{6,2},{7,3},{8,12},{9,13},{10,... | collective-permute-start | bytes 1769480 | tf_op jit(solution)/shard_map/ppermute | solution.py:630
  344.3 57.1 %collective-permute-start.71 = (bf16[4,192,384]{2,1,0:T(8,128)(2,1)S(1)}, bf16[4,192,384]{2,1,0:T(8,128)(2,1)S(1)}, u32[]{:S(2)}, u32[]{:S(2)}) collective-permute-start(bf16[4,192,384]{2,1,0:T(8,128)(2,1)S(1)} %dynamic-slice_bitcast_fusion.1), channel_id=1, source_target_pairs={{0,4},{1,5},{2,6},{3,7},{4,0},{5,1},{6,2},{7,3},{8,12},{9,13},{10,... | collective-permute-start | bytes 1769480 | tf_op jit(solution)/shard_map/ppermute | solution.py:630
  352.6 52.2 %collective-permute-start.66 = (bf16[4,96,768]{2,1,0:T(8,128)(2,1)S(1)}, bf16[4,96,768]{2,1,0:T(8,128)(2,1)S(1)}, u32[]{:S(2)}, u32[]{:S(2)}) collective-permute-start(bf16[4,96,768]{2,1,0:T(8,128)(2,1)S(1)} %dynamic-slice_bitcast_fusion.2), channel_id=1, source_target_pairs={{0,2},{1,3},{2,0},{3,1},{4,6},{5,7},{6,4},{7,5},{8,10},{9,11},{10,... | collective-permute-start | bytes 1769480 | tf_op jit(solution)/shard_map/ppermute | solution.py:630
  355.3 57.1 %collective-permute-start.76 = (bf16[4,192,384]{2,1,0:T(8,128)(2,1)S(1)}, bf16[4,192,384]{2,1,0:T(8,128)(2,1)S(1)}, u32[]{:S(2)}, u32[]{:S(2)}) collective-permute-start(bf16[4,192,384]{2,1,0:T(8,128)(2,1)S(1)} %dynamic-slice_bitcast_fusion), channel_id=1, source_target_pairs={{0,4},{1,5},{2,6},{3,7},{4,0},{5,1},{6,2},{7,3},{8,12},{9,13},{10,... | collective-permute-start | bytes 1769480 | tf_op jit(solution)/shard_map/ppermute | solution.py:630
  377.8 55.6 %collective-permute-start.60 = (bf16[4,96,768]{2,1,0:T(8,128)(2,1)S(1)}, bf16[4,96,768]{2,1,0:T(8,128)(2,1)S(1)}, u32[]{:S(2)}, u32[]{:S(2)}) collective-permute-start(bf16[4,96,768]{2,1,0:T(8,128)(2,1)S(1)} %dynamic-slice_bitcast_fusion.3), channel_id=1, source_target_pairs={{0,2},{1,3},{2,0},{3,1},{4,6},{5,7},{6,4},{7,5},{8,10},{9,11},{10,... | collective-permute-start | bytes 1769480 | tf_op jit(solution)/shard_map/ppermute | solution.py:630
  422.0 24.9 %collective-permute-start.68 = (bf16[96,768]{1,0:T(8,128)(2,1)S(1)}, bf16[96,768]{1,0:T(8,128)(2,1)S(1)}, u32[]{:S(2)}, u32[]{:S(2)}) collective-permute-start(bf16[96,768]{1,0:T(8,128)(2,1)S(1)} %get-tuple-element.185), channel_id=1, source_target_pairs={{0,16},{1,17},{2,18},{3,19},{4,20},{5,21},{6,22},{7,23},{8,24},{9,... | collective-permute-start | bytes 442376 | tf_op jit(solution)/shard_map/ppermute | solution.py:630
  433.4 26.1 %collective-permute-start.78 = (bf16[192,384]{1,0:T(8,128)(2,1)S(1)}, bf16[192,384]{1,0:T(8,128)(2,1)S(1)}, u32[]{:S(2)}, u32[]{:S(2)}) collective-permute-start(bf16[192,384]{1,0:T(8,128)(2,1)S(1)} %get-tuple-element.179), channel_id=1, source_target_pairs={{0,16},{1,17},{2,18},{3,19},{4,20},{5,21},{6,22},{7,23},{8,24},{9,... | collective-permute-start | bytes 442376 | tf_op jit(solution)/shard_map/ppermute | solution.py:630
  436.0 23.6 %collective-permute-start.77 = (bf16[192,384]{1,0:T(8,128)(2,1)S(1)}, bf16[192,384]{1,0:T(8,128)(2,1)S(1)}, u32[]{:S(2)}, u32[]{:S(2)}) collective-permute-start(bf16[192,384]{1,0:T(8,128)(2,1)S(1)} %get-tuple-element.177), channel_id=1, source_target_pairs={{0,8},{1,9},{2,10},{3,11},{4,12},{5,13},{6,14},{7,15},{8,16},{9,17... | collective-permute-start | bytes 442376 | tf_op jit(solution)/shard_map/ppermute | solution.py:630
  (182 other events, 1443.3 us)
